TPU v7x, 32 devices: a whole 2x2x4 slice. The times are simulated.
32 devices in a mesh: row: 4 (over y, core), col: 8 (over z, x).
Axes of the slice: x: 2, y: 2, z: 4, core: 2. Of those that a mesh axis runs over, the one named last changes fastest.
Arguments:
- features: bfloat16 [65536, 256], P(('row', 'col')), may hold values from -6 to 6
- hub_features: bfloat16 [512, 256], P(('row', 'col')), may hold values from -6 to 6
- w_self: bfloat16 [256, 256], replicated, may hold values from -0.375 to 0.375
- w_neigh: bfloat16 [256, 256], replicated, may hold values from -0.375 to 0.375
- out_bias: float32 [256], replicated, may hold values from -4 to 4
- local_edges: int32 [65536, 4], P(('row', 'col')), may hold values from 0 to 2047
- hub_edges: int32 [65536, 2], P(('row', 'col')), may hold values from 0 to 511
- remote_edges: int32 [65536, 4], P(('row', 'col')), may hold values from 0 to 511
- send_rows: int32 [32, 512], P(('row', 'col')), may hold values from 0 to 2047
- cotangent: bfloat16 [65536, 256], P(('row', 'col')), may hold values from -6 to 6
Outputs:
- activated: bfloat16 [65536, 256], P(('row', 'col'))
- grad_features: float32 [65536, 256], P(('row', 'col'))
- grad_hubs: float32 [512, 256], P(('row', 'col'))
- grad_w_self: float32 [256, 256], replicated
- grad_w_neigh: float32 [256, 256], replicated
- grad_bias: float32 [256], replicated
All inputs are finite; a program needn't handle non-finite values.
Results may differ from a plain program's by a relative error of at most 0.0075.
Values may be sent and summed in bfloat16 or wider, within the bound.
No kernel may reach another device: no remote copies, remote signals or barrier semaphores. Data moves between devices by JAX's collectives and lax.ppermute only.
A program may use at most 64 MiB of HBM per device.

v0:
```python
import math

import jax
import jax.numpy as jnp
from jax import lax
from jax.sharding import PartitionSpec as P


def edge_counts(edge_block, table_rows, dtype):
    index_row = jnp.arange(table_rows, dtype=jnp.int32)
    hits = edge_block[:, :, None] == index_row[None, None, :]
    return jnp.sum(hits.astype(dtype), axis=1)


def to_blocks(values, block_rows):
    return values.reshape((values.shape[0] // block_rows, block_rows) + values.shape[1:])


def add_transposed(total, counts, values):
    return total + lax.dot_general(
        counts,
        values,
        (((0,), (0,)), ((), ())),
        preferred_element_type=jnp.float32,
        precision=lax.Precision.HIGHEST,
    )


def body(
    features,
    hub_features,
    w_self,
    w_neigh,
    out_bias,
    local_edges,
    hub_edges,
    remote_edges,
    send_rows,
    cotangent,
):
    feat_width = features.shape[1]
    node_rows = features.shape[0]
    part_count = lax.axis_size(("row", "col"))
    slot_count = send_rows.shape[1] // part_count
    send_lists = send_rows.reshape(-1, 1)
    send_total = send_lists.shape[0]
    send_block = math.gcd(512, send_total)
    node_block = math.gcd(512, node_rows)

    def pick_rows(edge_block):
        counts = edge_counts(edge_block, node_rows, jnp.bfloat16)
        return jnp.dot(counts, features, preferred_element_type=jnp.float32).astype(jnp.bfloat16)

    outgoing = lax.map(pick_rows, to_blocks(send_lists, send_block)).reshape(
        part_count, slot_count, feat_width
    )
    incoming = lax.all_to_all(outgoing, ("row", "col"), split_axis=0, concat_axis=0, tiled=True)
    incoming = incoming.reshape(part_count * slot_count, feat_width)
    hub_all = lax.all_gather(hub_features, ("row", "col"), axis=0, tiled=True)
    hub_total_rows = hub_all.shape[0]
    remote_total = incoming.shape[0]
    fanout = local_edges.shape[1] + hub_edges.shape[1] + remote_edges.shape[1]
    edge_blocks = (
        to_blocks(local_edges, node_block),
        to_blocks(hub_edges, node_block),
        to_blocks(remote_edges, node_block),
    )

    def gather_block(edges):
        local_block, hub_block, remote_block = edges
        total = jnp.dot(
            edge_counts(local_block, node_rows, jnp.bfloat16),
            features,
            preferred_element_type=jnp.float32,
        )
        total = total + jnp.dot(
            edge_counts(hub_block, hub_total_rows, jnp.bfloat16),
            hub_all,
            preferred_element_type=jnp.float32,
        )
        total = total + jnp.dot(
            edge_counts(remote_block, remote_total, jnp.bfloat16),
            incoming,
            preferred_element_type=jnp.float32,
        )
        return total

    summed = lax.map(gather_block, edge_blocks).reshape(node_rows, feat_width)
    neighbour_mean = (summed / fanout).astype(jnp.bfloat16)
    pre_act = jnp.dot(features, w_self, preferred_element_type=jnp.float32)
    pre_act = pre_act + jnp.dot(neighbour_mean, w_neigh, preferred_element_type=jnp.float32)
    pre_act = pre_act + out_bias
    sigmoid_pre = jax.nn.sigmoid(pre_act)
    activated = (pre_act * sigmoid_pre).astype(jnp.bfloat16)
    grad_pre = (
        cotangent.astype(jnp.float32) * sigmoid_pre * (1.0 + pre_act * (1.0 - sigmoid_pre))
    ).astype(jnp.bfloat16)
    term_self = lax.dot_general(
        features, grad_pre, (((0,), (0,)), ((), ())), preferred_element_type=jnp.float32
    )
    term_neigh = lax.dot_general(
        neighbour_mean, grad_pre, (((0,), (0,)), ((), ())), preferred_element_type=jnp.float32
    )
    term_bias = jnp.sum(grad_pre.astype(jnp.float32), axis=0)
    grad_w_self, grad_w_neigh, grad_bias = lax.psum(
        (term_self, term_neigh, term_bias), ("row", "col")
    )
    grad_mean = (
        lax.dot_general(
            grad_pre, w_neigh, (((1,), (1,)), ((), ())), preferred_element_type=jnp.float32
        )
        / fanout
    )
    grad_direct = lax.dot_general(
        grad_pre, w_self, (((1,), (1,)), ((), ())), preferred_element_type=jnp.float32
    )

    def spread_block(carry, inputs):
        local_acc, hub_acc, remote_acc = carry
        local_block, hub_block, remote_block, mean_block = inputs
        local_acc = add_transposed(
            local_acc, edge_counts(local_block, node_rows, jnp.float32), mean_block
        )
        hub_acc = add_transposed(
            hub_acc, edge_counts(hub_block, hub_total_rows, jnp.float32), mean_block
        )
        remote_acc = add_transposed(
            remote_acc, edge_counts(remote_block, remote_total, jnp.float32), mean_block
        )
        return ((local_acc, hub_acc, remote_acc), None)

    start = (
        jnp.zeros((node_rows, feat_width), jnp.float32),
        jnp.zeros((hub_total_rows, feat_width), jnp.float32),
        jnp.zeros((remote_total, feat_width), jnp.float32),
    )
    (local_grad, hub_terms, grad_incoming), unused = lax.scan(
        spread_block, start, edge_blocks + (to_blocks(grad_mean, node_block),)
    )
    grad_features = grad_direct + local_grad
    returned = lax.all_to_all(
        grad_incoming.reshape(part_count, slot_count, feat_width).astype(jnp.bfloat16),
        ("row", "col"),
        split_axis=0,
        concat_axis=0,
        tiled=True,
    ).astype(jnp.float32)
    returned = returned.reshape(part_count * slot_count, feat_width)

    def return_block(total, inputs):
        list_block, grad_block = inputs
        return (
            add_transposed(total, edge_counts(list_block, node_rows, jnp.float32), grad_block),
            None,
        )

    grad_features, unused = lax.scan(
        return_block,
        grad_features,
        (to_blocks(send_lists, send_block), to_blocks(returned, send_block)),
    )
    hub_own = hub_features.shape[0]
    hub_summed = lax.psum(hub_terms, ("row", "col"))
    grad_hubs = lax.dynamic_slice_in_dim(
        hub_summed, lax.axis_index(("row", "col")) * hub_own, hub_own, 0
    )
    return (activated, grad_features, grad_hubs, grad_w_self, grad_w_neigh, grad_bias)


def solution(mesh):
    placed = (
        P(("row", "col"), None),
        P(("row", "col"), None),
        P(),
        P(),
        P(),
        P(("row", "col"), None),
        P(("row", "col"), None),
        P(("row", "col"), None),
        P(("row", "col"), None),
        P(("row", "col"), None),
    )
    return jax.shard_map(
        body,
        mesh=mesh,
        in_specs=placed,
        out_specs=(
            P(("row", "col"), None),
            P(("row", "col"), None),
            P(("row", "col"), None),
            P(),
            P(),
            P(),
        ),
        check_vma=False,
    )
```

profile of v0, /device:TPU:0, one launch (start us, length us, event | category | flops | bytes accessed | tf_op | source)
XLA Modules:
  0.0 354.0 jit_solution(15013578368478612162)
XLA Ops:
  7.2 2.9 fusion.28
  10.1 7.3 %all-to-all-start = ((bf16[32,16,256]{2,1,0:T(8,128)(2,1)}), bf16[32,16,256]{2,1,0:T(8,128)(2,1)S(1)}, u32[]{:S(2)}, u32[]{:S(2)}) async-start(bf16[32,16,256]{2,1,0:T(8,128)(2,1)} %bitcast.8), calls=%async_computation | async-start | bytes 524288 | tf_op jit(solution)/shard_map/all_to_all | solution.py:57
  17.5 75.0 %all_gather.3 = bf16[512,256]{1,0:T(8,128)(2,1)} all-gather(bf16[16,256]{1,0:T(8,128)(2,1)} %param.15), channel_id=1, replica_groups=mesh['row'=4,'col'=8] {'row','col'}, dimensions={0}, use_global_device_ids=true | all-gather | bytes 270336 | tf_op jit(solution)/shard_map/all_gather | solution.py:59
  92.5 2.7 fusion.31
  95.2 24.8 %while.36 = (s32[]{:T(128)}, f32[4,512,256]{2,1,0:T(8,128)}, s32[4,512,4]{1,2,0:T(4,128)}, bf16[2048,256]{1,0:T(8,128)(2,1)S(1)}, s32[4,512,2]{1,2,0:T(2,128)S(1...) while((s32[]{:T(128)}, f32[4,512,256]{2,1,0:T(8,128)}, ...), condition=%wide.region_4.5_spmd, body=%wide.region_0.0_spmd.sunk | while | flops 821297152 | bytes 11595917 | solution.py:88
  97.5 2.3 fusion.84
  103.7 2.3 fusion.84
  109.9 2.3 fusion.84
  116.1 2.3 fusion.84
  120.0 2.0 multiply_convert_fusion.2
  122.5 2.8 convert_reduce_fusion.3
  128.2 70.6 %while.37 = (s32[]{:T(128)}, f32[2048,256]{1,0:T(8,128)S(1)}, f32[512,256]{1,0:T(8,128)}, f32[512,256]{1,0:T(8,128)}, s32[4,512,4]{1,2,0:T(4,128)}, /*index=5*/f...) while((s32[]{:T(128)}, f32[2048,256]{1,0:T(8,128)S(1)}, ...), condition=%wide.region_9.10_spmd.clone, body=%wide.region_5.0_spmd.clone.sunk | while | flops 4849139712 | bytes 33091808 | solution.py:137
  129.2 3.8 %convolution_add_fusion.10 = f32[512,256]{1,0:T(8,128)} fusion(f32[512,512]{1,0:T(8,128)S(1)} %convert_reduce_fusion.8, f32[512,256]{1,0:T(8,128)} %get-tuple-element.434, f32[4,512,256]{2,1,0:T(8,128)} %get-tuple-element.447, s32[]{:T(128)S(6)} %copy.36, pred[]{:T(512)S(6)} %compare.3), kind=kOutput, calls=%fused_computation.24.clone.1 | convolution fusion | flops 805568512 | bytes 2621445 | tf_op jit(solution)/shard_map/while/body/eval_jaxpr/dot_general | solution.py:20
  133.7 2.0 convolution_add_fusion.11
  135.7 2.1 convert_reduce_fusion.7
  137.8 7.9 %convolution_add_fusion.9 = f32[2048,256]{1,0:T(8,128)S(1)} fusion(f32[512,2048]{1,0:T(8,128)S(1)} %convert_reduce_fusion.7, f32[2048,256]{1,0:T(8,128)S(1)} %get-tuple-element.433, pred[]{:T(512)S(6)} %compare.3, f32[4,512,256]{2,1,0:T(8,128)S(1)} %copy-done.2, s32[]{:T(128)S(6)} %copy.36), kind=kOutput, calls=%fused_computation.20.clone.1 | convolution fusion | flops 3222274048 | bytes 8912901 | tf_op jit(solution)/shard_map/while/body/eval_jaxpr/dot_general | solution.py:20
  146.7 4.0 %convolution_add_fusion.10 = f32[512,256]{1,0:T(8,128)} fusion(f32[512,512]{1,0:T(8,128)S(1)} %convert_reduce_fusion.8, f32[512,256]{1,0:T(8,128)} %get-tuple-element.434, f32[4,512,256]{2,1,0:T(8,128)} %get-tuple-element.447, s32[]{:T(128)S(6)} %copy.36, pred[]{:T(512)S(6)} %compare.3), kind=kOutput, calls=%fused_computation.24.clone.1 | convolution fusion | flops 805568512 | bytes 2621445 | tf_op jit(solution)/shard_map/while/body/eval_jaxpr/dot_general | solution.py:20
  151.3 2.0 convolution_add_fusion.11
  153.3 2.1 convert_reduce_fusion.7
  155.4 7.9 %convolution_add_fusion.9 = f32[2048,256]{1,0:T(8,128)S(1)} fusion(f32[512,2048]{1,0:T(8,128)S(1)} %convert_reduce_fusion.7, f32[2048,256]{1,0:T(8,128)S(1)} %get-tuple-element.433, pred[]{:T(512)S(6)} %compare.3, f32[4,512,256]{2,1,0:T(8,128)S(1)} %copy-done.2, s32[]{:T(128)S(6)} %copy.36), kind=kOutput, calls=%fused_computation.20.clone.1 | convolution fusion | flops 3222274048 | bytes 8912901 | tf_op jit(solution)/shard_map/while/body/eval_jaxpr/dot_general | solution.py:20
  164.3 4.0 %convolution_add_fusion.10 = f32[512,256]{1,0:T(8,128)} fusion(f32[512,512]{1,0:T(8,128)S(1)} %convert_reduce_fusion.8, f32[512,256]{1,0:T(8,128)} %get-tuple-element.434, f32[4,512,256]{2,1,0:T(8,128)} %get-tuple-element.447, s32[]{:T(128)S(6)} %copy.36, pred[]{:T(512)S(6)} %compare.3), kind=kOutput, calls=%fused_computation.24.clone.1 | convolution fusion | flops 805568512 | bytes 2621445 | tf_op jit(solution)/shard_map/while/body/eval_jaxpr/dot_general | solution.py:20
  171.0 2.1 convert_reduce_fusion.7
  173.1 7.9 %convolution_add_fusion.9 = f32[2048,256]{1,0:T(8,128)S(1)} fusion(f32[512,2048]{1,0:T(8,128)S(1)} %convert_reduce_fusion.7, f32[2048,256]{1,0:T(8,128)S(1)} %get-tuple-element.433, pred[]{:T(512)S(6)} %compare.3, f32[4,512,256]{2,1,0:T(8,128)S(1)} %copy-done.2, s32[]{:T(128)S(6)} %copy.36), kind=kOutput, calls=%fused_computation.20.clone.1 | convolution fusion | flops 3222274048 | bytes 8912901 | tf_op jit(solution)/shard_map/while/body/eval_jaxpr/dot_general | solution.py:20
  182.0 4.0 %convolution_add_fusion.10 = f32[512,256]{1,0:T(8,128)} fusion(f32[512,512]{1,0:T(8,128)S(1)} %convert_reduce_fusion.8, f32[512,256]{1,0:T(8,128)} %get-tuple-element.434, f32[4,512,256]{2,1,0:T(8,128)} %get-tuple-element.447, s32[]{:T(128)S(6)} %copy.36, pred[]{:T(512)S(6)} %compare.3), kind=kOutput, calls=%fused_computation.24.clone.1 | convolution fusion | flops 805568512 | bytes 2621445 | tf_op jit(solution)/shard_map/while/body/eval_jaxpr/dot_general | solution.py:20
  188.6 2.1 convert_reduce_fusion.7
  190.7 7.9 %convolution_add_fusion.9 = f32[2048,256]{1,0:T(8,128)S(1)} fusion(f32[512,2048]{1,0:T(8,128)S(1)} %convert_reduce_fusion.7, f32[2048,256]{1,0:T(8,128)S(1)} %get-tuple-element.433, pred[]{:T(512)S(6)} %compare.3, f32[4,512,256]{2,1,0:T(8,128)S(1)} %copy-done.2, s32[]{:T(128)S(6)} %copy.36), kind=kOutput, calls=%fused_computation.20.clone.1 | convolution fusion | flops 3222274048 | bytes 8912901 | tf_op jit(solution)/shard_map/while/body/eval_jaxpr/dot_general | solution.py:20
  200.6 2.7 all-to-all-start.1
  203.4 2.4 convolution_bitcast_fusion
  205.8 40.8 %psum.31 = f32[256]{0:T(256)} all-reduce(f32[256]{0:T(256)S(1)} %copy-done.10), channel_id=1, replica_groups=mesh['row'=4,'col'=8] {'row','col'}, use_global_device_ids=true, to_apply=%region_14.15 | all-reduce | flops 256 | bytes 2048 | tf_op jit(solution)/shard_map/psum | solution.py:105
  246.7 3.0 convolution_add_fusion.4
  249.7 4.3 %fusion.22 = f32[2048,256]{1,0:T(8,128)} fusion(f32[2048,256]{1,0:T(8,128)} %convolution_add_fusion.4, bf16[512,256]{1,0:T(8,128)(2,1)S(1)} %bitcast.101, s32[512]{0:T(512)S(1)} %bitcast.107), kind=kOutput, calls=%fused_computation.42 | convolution fusion | flops 538443776 | bytes 4458496 | tf_op jit(solution)/shard_map/while/body/eval_jaxpr/dot_general | solution.py:20
  254.0 88.4 %all-reduce.3.cloned.1.call-done = (f32[512,256]{1,0:T(8,128)}, f32[256,256]{0,1:T(8,128)}, f32[256,256]{1,0:T(8,128)}) async-done(((f32[512,256]{1,0:T(8,128)}, f32[256,256]{0,1:T(8,128)}, f32[256,256]{1,0:T(8,128)}), (f32[512,256]{1,0:T(8,128)}, f32[256,256]{0,1:T(8,128)}, f32[256,256]{1,0:T(8,128)})) %all-reduce.3.cloned.1.call-update) | async-done | bytes 1048592 | tf_op jit(solution)/shard_map/psum | solution.py:163
  (110 shorter events, 35.9 us)
Async XLA Ops:
  7.2 114.8 %copy-start = (bf16[256,256]{1,0:T(8,128)(2,1)S(1)}, bf16[256,256]{1,0:T(8,128)(2,1)}, u32[]{:S(2)}) copy-start(bf16[256,256]{1,0:T(8,128)(2,1)} %param.17) | copy-start | bytes 393220
  7.2 85.3 %copy-start.1 = (bf16[2048,256]{1,0:T(8,128)(2,1)S(1)}, bf16[2048,256]{1,0:T(8,128)(2,1)}, u32[]{:S(2)}) copy-start(bf16[2048,256]{1,0:T(8,128)(2,1)} %param.14) | copy-start | bytes 3145732
  10.1 85.1 %copy-start.8 = (s32[2048,2]{0,1:T(2,128)S(1)}, s32[2048,2]{0,1:T(2,128)}, u32[]{:S(2)}) copy-start(s32[2048,2]{0,1:T(2,128)} %param.20) | copy-start | bytes 49156
  10.1 85.1 %all-to-all-start = ((bf16[32,16,256]{2,1,0:T(8,128)(2,1)}), bf16[32,16,256]{2,1,0:T(8,128)(2,1)S(1)}, u32[]{:S(2)}, u32[]{:S(2)}) async-start(bf16[32,16,256]{2,1,0:T(8,128)(2,1)} %bitcast.8), calls=%async_computation | async-start | bytes 524288 | tf_op jit(solution)/shard_map/all_to_all | solution.py:57
  95.2 2.1 copy-start.6
  101.4 2.0 copy-start.6
  107.6 2.0 copy-start.6
  113.8 2.0 copy-start.6
  120.0 2.2 copy-start.7
  120.0 2.5 copy-start.11
  120.0 2.5 copy-start.12
  125.2 3.0 copy-start.5
  129.2 4.5 %copy-start.2 = (f32[4,512,256]{2,1,0:T(8,128)S(1)}, f32[4,512,256]{2,1,0:T(8,128)}, u32[]{:S(2)}) copy-start(f32[4,512,256]{2,1,0:T(8,128)} %get-tuple-element.447) | copy-start | bytes 6291460 | tf_op jit(solution)/shard_map/while
  129.2 4.5 %copy-start.3 = (f32[512,256]{1,0:T(8,128)S(1)}, f32[512,256]{1,0:T(8,128)}, u32[]{:S(2)}) copy-start(f32[512,256]{1,0:T(8,128)} %get-tuple-element.435) | copy-start | bytes 1572868 | tf_op jit(solution)/shard_map/while
  135.7 2.1 copy-start.4
  146.7 4.7 %copy-start.2 = (f32[4,512,256]{2,1,0:T(8,128)S(1)}, f32[4,512,256]{2,1,0:T(8,128)}, u32[]{:S(2)}) copy-start(f32[4,512,256]{2,1,0:T(8,128)} %get-tuple-element.447) | copy-start | bytes 6291460 | tf_op jit(solution)/shard_map/while
  146.7 4.7 %copy-start.3 = (f32[512,256]{1,0:T(8,128)S(1)}, f32[512,256]{1,0:T(8,128)}, u32[]{:S(2)}) copy-start(f32[512,256]{1,0:T(8,128)} %get-tuple-element.435) | copy-start | bytes 1572868 | tf_op jit(solution)/shard_map/while
  153.3 2.1 copy-start.4
  164.3 4.7 %copy-start.2 = (f32[4,512,256]{2,1,0:T(8,128)S(1)}, f32[4,512,256]{2,1,0:T(8,128)}, u32[]{:S(2)}) copy-start(f32[4,512,256]{2,1,0:T(8,128)} %get-tuple-element.447) | copy-start | bytes 6291460 | tf_op jit(solution)/shard_map/while
  164.3 4.7 %copy-start.3 = (f32[512,256]{1,0:T(8,128)S(1)}, f32[512,256]{1,0:T(8,128)}, u32[]{:S(2)}) copy-start(f32[512,256]{1,0:T(8,128)} %get-tuple-element.435) | copy-start | bytes 1572868 | tf_op jit(solution)/shard_map/while
  171.0 2.1 copy-start.4
  182.0 4.7 %copy-start.2 = (f32[4,512,256]{2,1,0:T(8,128)S(1)}, f32[4,512,256]{2,1,0:T(8,128)}, u32[]{:S(2)}) copy-start(f32[4,512,256]{2,1,0:T(8,128)} %get-tuple-element.447) | copy-start | bytes 6291460 | tf_op jit(solution)/shard_map/while
  182.0 4.7 %copy-start.3 = (f32[512,256]{1,0:T(8,128)S(1)}, f32[512,256]{1,0:T(8,128)}, u32[]{:S(2)}) copy-start(f32[512,256]{1,0:T(8,128)} %get-tuple-element.435) | copy-start | bytes 1572868 | tf_op jit(solution)/shard_map/while
  188.6 2.1 copy-start.4
  200.6 5.2 %copy-start.10 = (f32[256]{0:T(256)S(1)}, f32[256]{0:T(256)}, u32[]{:S(2)}) copy-start(f32[256]{0:T(256)} %get-tuple-element.282) | copy-start | bytes 3076
  200.6 49.1 %all-to-all-start.1 = ((bf16[32,16,256]{2,1,0:T(8,128)(2,1)}), bf16[32,16,256]{2,1,0:T(8,128)(2,1)S(1)}, u32[]{:S(2)}, u32[]{:S(2)}) async-start(bf16[32,16,256]{2,1,0:T(8,128)(2,1)} %bitcast.102), calls=%async_computation.1 | async-start | bytes 524288 | tf_op jit(solution)/shard_map/all_to_all | solution.py:141
  203.4 139.1 %all-reduce.3.cloned.1.call-start = ((), (), s32[]{:S(2)}) async-start(), calls=%async_computation.2 | async-start | bytes 2097152 | tf_op jit(solution)/shard_map/psum | solution.py:163
  246.7 3.0 copy-start.9
Sparse Core Ops, SparseCore 0:
  210.3 132.0 all-reduce.2
where the time goes:
time: 355 us; the launch traced here: 354 us
  blocking collectives  116 us (33%)
  waiting for transfers between devices  88.4 us (25%)
  matrix products  84.6 us (24%)
  other arithmetic  28.7 us (8%)
  between operations  14.1 us (4%)
  local copies, waits for them, and re-layouts  11.3 us (3%)
  starting transfers between devices  10.1 us (3%)
    psum x1, waiting for transfers between devices, body(): hub_summed = lax.psum(hub_terms, ('row', 'col'))  88.4 us
    all_gather x1, blocking collectives, body(): hub_all = lax.all_gather(hub_features, ('row', 'col'), axis=0, tiled=True)  75 us
    dot_general x13, matrix products, add_transposed(): lax.dot_general(counts, values, (((0,), (0,)), ((), ())), preferred_eleme...  59.4 us
    psum x1, blocking collectives, body(): lax.psum((term_self, term_neigh, term_bias), ('row', 'col'))  40.8 us
    reduce_sum x24, other arithmetic, edge_counts(): return jnp.sum(hits.astype(dtype), axis=1)  25 us
    all_to_all x1, starting transfers between devices, body(): lax.all_to_all(outgoing, ('row', 'col'), split_axis=0, concat_axis=0, til...  7.3 us
  transfers between devices with their start and end apart: 3, of which 1 were waited for; matrix products, arithmetic and copies ran while one was open for 3% of the time, Pallas kernels for 0%

commit v1 on v0

v1 whole, which is shorter than its diff:
```python
import functools

import jax
import jax.numpy as jnp
from jax import lax
from jax.experimental import pallas as pl
from jax.experimental.pallas import tpu as pltpu
from jax.sharding import PartitionSpec as P

AXES = ("row", "col")
LANES = 128
VMEM_LIMIT = 44 * 1024 * 1024
NT = (((1,), (1,)), ((), ()))
TN = (((0,), (0,)), ((), ()))


def params():
    return pltpu.CompilerParams(vmem_limit_bytes=VMEM_LIMIT)


def cost(flops, moved):
    return pl.CostEstimate(flops=int(flops), bytes_accessed=int(moved), transcendentals=0)


def full(shape):
    return pl.BlockSpec(shape, lambda *_: (0,) * len(shape))


def along_rows(index_row):
    count = index_row.shape[1]
    return jnp.transpose(jnp.broadcast_to(index_row, (LANES, count))).astype(jnp.int16)


def hits_by_row(columns, first, width):
    rows = columns[0].shape[0]
    lane = lax.broadcasted_iota(jnp.int32, (rows, LANES), 1).astype(jnp.int16)
    one = jnp.ones((rows, LANES), jnp.bfloat16)
    zero = jnp.zeros((rows, LANES), jnp.bfloat16)
    tiles = []
    for start in range(first, first + width, LANES):
        here = lane + jnp.int16(start)
        total = None
        for column in columns:
            hit = jnp.where(column == here, one, zero)
            total = hit if total is None else total + hit
        tiles.append(total)
    return jnp.concatenate(tiles, axis=1) if len(tiles) > 1 else tiles[0]


def hits_by_column(index_rows, first, height):
    count = index_rows[0].shape[1]
    down = lax.broadcasted_iota(jnp.int32, (height, count), 0).astype(jnp.int16)
    one = jnp.ones((height, count), jnp.bfloat16)
    zero = jnp.zeros((height, count), jnp.bfloat16)
    total = None
    for row in index_rows:
        entry = jnp.broadcast_to(row - first, (16, count)).astype(jnp.int16)
        entry = jnp.broadcast_to(entry[None], (height // 16, 16, count)).reshape(height, count)
        hit = jnp.where(entry == down, one, zero)
        total = hit if total is None else total + hit
    return total


def dot(a, b, dims=(((1,), (0,)), ((), ()))):
    return lax.dot_general(a, b, dims, preferred_element_type=jnp.float32)


def pick_kernel(send_ref, feat_ref, hub_ref, out_ref):
    parts, slab, width = out_ref.shape
    hub_rows = hub_ref.shape[0]
    slots = slab - hub_rows
    total = send_ref.shape[1]
    step = min(512, total)
    for start in range(0, total, step):
        column = along_rows(send_ref[:, start : start + step])
        picked = dot(hits_by_row([column], 0, feat_ref.shape[0]), feat_ref[...])
        out_ref[start // slots : (start + step) // slots, :slots, :] = (
            picked.astype(jnp.bfloat16).reshape(step // slots, slots, width)
        )
    out_ref[:, slots:, :] = jnp.broadcast_to(hub_ref[...][None], (parts, hub_rows, width))


def table_rows_of(hub_ref, remote_ref, slots, hub_rows):
    rows = []
    for j in range(remote_ref.shape[0]):
        entry = remote_ref[j : j + 1, :]
        rows.append(entry + lax.div(entry, jnp.int32(slots)) * hub_rows)
    for j in range(hub_ref.shape[0]):
        entry = hub_ref[j : j + 1, :]
        rows.append(entry + (lax.div(entry, jnp.int32(hub_rows)) + 1) * slots)
    return rows


def local_kernel(slots, hub_rows, local_ref, hub_ref, remote_ref, feat_ref, sum_ref, by_row_ref, by_col_ref):
    tile = 256
    local_rows = [local_ref[j : j + 1, :] for j in range(local_ref.shape[0])]
    columns = [along_rows(row) for row in local_rows]
    total = None
    for start in range(0, feat_ref.shape[0], tile):
        part = dot(hits_by_row(columns, start, tile), feat_ref[start : start + tile, :])
        total = part if total is None else total + part
    sum_ref[...] = total
    table = table_rows_of(hub_ref, remote_ref, slots, hub_rows)
    columns = [along_rows(row) for row in table]
    for start in range(0, by_row_ref.shape[1], tile):
        by_row_ref[:, start : start + tile] = hits_by_row(columns, start, tile)
        by_col_ref[start : start + tile, :] = hits_by_column(table, start, tile)


def middle_kernel(
    fanout,
    slots,
    feat_ref,
    sum_ref,
    by_row_ref,
    by_col_ref,
    table_ref,
    cot_ref,
    ws_ref,
    wn_ref,
    bias_ref,
    act_ref,
    grad_ref,
    pay_ref,
    table_acc,
    weight_acc,
    bias_acc,
):
    step = pl.program_id(0)
    width = feat_ref.shape[1]
    parts, slab, _ = table_ref.shape

    @pl.when(step == 0)
    def _():
        table_acc[...] = jnp.zeros_like(table_acc)
        weight_acc[...] = jnp.zeros_like(weight_acc)
        bias_acc[...] = jnp.zeros_like(bias_acc)

    feat = feat_ref[...]
    table = table_ref[...].reshape(parts * slab, width)
    mean = ((sum_ref[...] + dot(by_row_ref[...], table)) / fanout).astype(jnp.bfloat16)
    pre = dot(feat, ws_ref[...]) + dot(mean, wn_ref[...]) + bias_ref[...]
    sig = jax.nn.sigmoid(pre)
    act_ref[...] = (pre * sig).astype(jnp.bfloat16)
    grad = (cot_ref[...].astype(jnp.float32) * sig * (1.0 + pre * (1.0 - sig))).astype(jnp.bfloat16)
    grad_ref[...] = grad
    table_acc[...] += dot(by_col_ref[...], grad)
    weight_acc[:width, :] += dot(feat, grad, TN)
    weight_acc[width:, :] += dot(mean, grad, TN)
    bias_acc[...] += jnp.sum(grad.astype(jnp.float32), axis=0, keepdims=True)

    @pl.when(step == pl.num_programs(0) - 1)
    def _():
        pay_ref[:, :slab, :] = table_acc[...].astype(jnp.bfloat16).reshape(parts, slab, width)
        holders = 2 * width // 16
        pay_ref[:holders, slab : slab + 16, :] = (
            weight_acc[...].astype(jnp.bfloat16).reshape(holders, 16, width)
        )
        if parts > holders:
            pay_ref[holders:, slab : slab + 16, :] = jnp.zeros((parts - holders, 16, width), jnp.bfloat16)
        whole = bias_acc[...]
        high = whole.astype(jnp.bfloat16).astype(jnp.float32)
        place = lax.broadcasted_iota(jnp.int32, (8, width), 0)
        rows = jnp.where(place == 0, high, jnp.where(place == 1, whole - high, 0.0)).astype(jnp.bfloat16)
        pay_ref[:, slab + 16 :, :] = jnp.broadcast_to(rows[None], (parts, 8, width))


def scatter_kernel(local_ref, grad_ref, out_ref):
    height = out_ref.shape[0]
    first = pl.program_id(0) * height
    total = None
    for start in range(0, grad_ref.shape[0], 256):
        rows = [local_ref[j : j + 1, start : start + 256] for j in range(local_ref.shape[0])]
        part = dot(hits_by_column(rows, first, height), grad_ref[start : start + 256, :])
        total = part if total is None else total + part
    out_ref[...] = total


def sums_kernel(fanout, slots, hub_rows, back_ref, wn_ref, weight_ref, bias_ref, hub_ref):
    slab = slots + hub_rows
    parts, _, width = back_ref.shape
    weight = jnp.sum(back_ref[:, slab : slab + 16, :].astype(jnp.float32), axis=0)
    weight_ref[...] = jnp.broadcast_to(weight.astype(jnp.bfloat16)[None], (parts, 16, width))
    tail = jnp.sum(back_ref[:, slab + 16 :, :].astype(jnp.float32), axis=0)
    bias_ref[...] = jnp.sum(tail, axis=0, keepdims=True)
    hub = jnp.sum(back_ref[:, slots:slab, :].astype(jnp.float32), axis=0)
    high = hub.astype(jnp.bfloat16)
    low = (hub - high.astype(jnp.float32)).astype(jnp.bfloat16)
    hub_ref[...] = (dot(high, wn_ref[...], NT) + dot(low, wn_ref[...], NT)) / fanout


def final_kernel(fanout, slots, send_ref, back_ref, scat_ref, grad_ref, ws_ref, wn_ref, out_ref):
    height, width = out_ref.shape
    first = pl.program_id(0) * height
    parts = back_ref.shape[0]
    returned = back_ref[:, :slots, :].reshape(parts * slots, width)
    total = scat_ref[...]
    count = send_ref.shape[1]
    for start in range(0, count, 512):
        stop = min(count, start + 512)
        total = total + dot(hits_by_column([send_ref[:, start:stop]], first, height), returned[start:stop, :])
    out_ref[...] = dot(grad_ref[...], ws_ref[...], NT) + dot((total / fanout).astype(jnp.bfloat16), wn_ref[...], NT)


def body(
    features,
    hub_features,
    w_self,
    w_neigh,
    out_bias,
    local_edges,
    hub_edges,
    remote_edges,
    send_rows,
    cotangent,
):
    nodes, width = features.shape
    hub_rows = hub_features.shape[0]
    parts = lax.axis_size(AXES)
    slots = send_rows.shape[1] // parts
    slab = slots + hub_rows
    table_rows = parts * slab
    fanout = float(local_edges.shape[1] + hub_edges.shape[1] + remote_edges.shape[1])
    bf16, f32 = jnp.bfloat16, jnp.float32
    local_t, hub_t, remote_t = local_edges.T, hub_edges.T, remote_edges.T
    bias = out_bias.reshape(1, width)

    def exchange(value):
        return lax.all_to_all(value, AXES, split_axis=0, concat_axis=0, tiled=True)

    payload = pl.pallas_call(
        pick_kernel,
        out_shape=jax.ShapeDtypeStruct((parts, slab, width), bf16),
        compiler_params=params(),
        cost_estimate=cost(2 * parts * slots * nodes * width, nodes * width * 2),
        name="pick_rows",
    )(send_rows, features, hub_features)
    table = exchange(payload)

    block = 256
    local_sum, by_row, by_col = pl.pallas_call(
        functools.partial(local_kernel, slots, hub_rows),
        grid=(nodes // block,),
        in_specs=[
            pl.BlockSpec((local_t.shape[0], block), lambda i: (0, i)),
            pl.BlockSpec((hub_t.shape[0], block), lambda i: (0, i)),
            pl.BlockSpec((remote_t.shape[0], block), lambda i: (0, i)),
            full((nodes, width)),
        ],
        out_specs=[
            pl.BlockSpec((block, width), lambda i: (i, 0)),
            pl.BlockSpec((block, table_rows), lambda i: (i, 0)),
            pl.BlockSpec((table_rows, block), lambda i: (0, i)),
        ],
        out_shape=[
            jax.ShapeDtypeStruct((nodes, width), f32),
            jax.ShapeDtypeStruct((nodes, table_rows), bf16),
            jax.ShapeDtypeStruct((table_rows, nodes), bf16),
        ],
        compiler_params=params(),
        cost_estimate=cost(8 * nodes * nodes * width, nodes * table_rows * 4),
        name="local_gather",
    )(local_t, hub_t, remote_t, features)

    block = 512
    activated, grad_pre, terms = pl.pallas_call(
        functools.partial(middle_kernel, fanout, slots),
        grid=(nodes // block,),
        in_specs=[
            pl.BlockSpec((block, width), lambda i: (i, 0)),
            pl.BlockSpec((block, width), lambda i: (i, 0)),
            pl.BlockSpec((block, table_rows), lambda i: (i, 0)),
            pl.BlockSpec((table_rows, block), lambda i: (0, i)),
            full((parts, slab, width)),
            pl.BlockSpec((block, width), lambda i: (i, 0)),
            full((width, width)),
            full((width, width)),
            full((1, width)),
        ],
        out_specs=[
            pl.BlockSpec((block, width), lambda i: (i, 0)),
            pl.BlockSpec((block, width), lambda i: (i, 0)),
            full((parts, slab + 24, width)),
        ],
        out_shape=[
            jax.ShapeDtypeStruct((nodes, width), bf16),
            jax.ShapeDtypeStruct((nodes, width), bf16),
            jax.ShapeDtypeStruct((parts, slab + 24, width), bf16),
        ],
        scratch_shapes=[
            pltpu.VMEM((table_rows, width), f32),
            pltpu.VMEM((2 * width, width), f32),
            pltpu.VMEM((1, width), f32),
        ],
        compiler_params=params(),
        cost_estimate=cost(4 * nodes * table_rows * width, nodes * table_rows * 4),
        name="activate",
    )(features, local_sum, by_row, by_col, table, cotangent, w_self, w_neigh, bias)
    back = exchange(terms)

    block = 256
    local_back = pl.pallas_call(
        scatter_kernel,
        grid=(nodes // block,),
        in_specs=[full(local_t.shape), full((nodes, width))],
        out_specs=pl.BlockSpec((block, width), lambda i: (i, 0)),
        out_shape=jax.ShapeDtypeStruct((nodes, width), f32),
        compiler_params=params(),
        cost_estimate=cost(8 * nodes * nodes * width, nodes * width * 6),
        name="local_scatter",
    )(local_t, grad_pre)

    weight_rows, grad_bias, grad_hubs = pl.pallas_call(
        functools.partial(sums_kernel, fanout, slots, hub_rows),
        out_shape=[
            jax.ShapeDtypeStruct((parts, 16, width), bf16),
            jax.ShapeDtypeStruct((1, width), f32),
            jax.ShapeDtypeStruct((hub_rows, width), f32),
        ],
        compiler_params=params(),
        cost_estimate=cost(0, parts * 72 * width * 2),
        name="sums",
    )(back, w_neigh)
    weights = exchange(weight_rows)

    block = 512
    grad_features = pl.pallas_call(
        functools.partial(final_kernel, fanout, slots),
        grid=(nodes // block,),
        in_specs=[
            full(send_rows.shape),
            full((parts, slab + 24, width)),
            pl.BlockSpec((block, width), lambda i: (i, 0)),
            pl.BlockSpec((block, width), lambda i: (i, 0)),
            full((width, width)),
            full((width, width)),
        ],
        out_specs=pl.BlockSpec((block, width), lambda i: (i, 0)),
        out_shape=jax.ShapeDtypeStruct((nodes, width), f32),
        compiler_params=params(),
        cost_estimate=cost(2 * nodes * parts * slots * width, nodes * width * 10),
        name="return_scatter",
    )(send_rows, back, local_back, grad_pre, w_self, w_neigh)

    weights = weights[: 2 * width // 16].reshape(2, width, width).astype(f32)
    return (activated, grad_features, grad_hubs, weights[0], weights[1], grad_bias.reshape(width))


def solution(mesh):
    split = P(AXES, None)
    return jax.shard_map(
        body,
        mesh=mesh,
        in_specs=(split, split, P(), P(), P(), split, split, split, split, split),
        out_specs=(split, split, split, P(), P(), P()),
        check_vma=False,
    )
```

time: 355 us -> 84.2 us (0.24)
  blocking collectives: 116 us -> 27.8 us
  matrix products: 84.6 us -> 0 us
  waiting for transfers between devices: 88.4 us -> 5.11 us
  Pallas kernels: 0 us -> 30 us
  other arithmetic: 28.7 us -> 0 us
  between operations: 14.1 us -> 0.75 us
    psum x1 -> x0, waiting for transfers between devices: 88.4 us -> none  [body(): hub_summed = lax.psum(hub_terms, ('row', 'col'))]
    dot_general x32 -> x0, matrix products: 84.6 us -> none  [the longest x13 59.4 us: add_transposed(): lax.dot_general(counts, values, (((0,), (0,)), ((), ())), preferred_eleme...]
    all_gather x1 -> x0, blocking collectives: 75 us -> none  [body(): hub_all = lax.all_gather(hub_features, ('row', 'col'), axis=0, tiled=True)]
    psum x1 -> x0, blocking collectives: 40.8 us -> none  [body(): lax.psum((term_self, term_neigh, term_bias), ('row', 'col'))]
    pallas_call x0 -> x6, Pallas kernels: none -> 30 us  [the longest x1 10.4 us: body(): pl.pallas_call(functools.partial(local_kernel, slots, hub_rows), grid=(no...]
    all_to_all x0 -> x1, blocking collectives: none -> 27.8 us  [exchange(): return lax.all_to_all(value, AXES, split_axis=0, concat_axis=0, tiled=True)]
    reduce_sum x24 -> x0, other arithmetic: 25 us -> none  [edge_counts(): return jnp.sum(hits.astype(dtype), axis=1)]
    eq x16 -> x0, local copies, waits for them, and re-layouts: 5.96 us -> none  [edge_counts(): hits = edge_block[:, :, None] == index_row[None, None, :]]
  transfers between devices with their start and end apart: 3 -> 2, of which waited for: 1 -> 2; matrix products, arithmetic and copies ran while one was open for 3% -> 0% of each run, Pallas kernels for 0% -> 22%
where the time goes in v1:
time: 84.2 us; the launch traced here: 83.7 us
  Pallas kernels  30 us (36%)
  blocking collectives  27.8 us (33%)
  local copies, waits for them, and re-layouts  10.1 us (12%)
  starting transfers between devices  9.88 us (12%)
  waiting for transfers between devices  5.11 us (6%)
    all_to_all x1, blocking collectives, exchange(): return lax.all_to_all(value, AXES, split_axis=0, concat_axis=0, tiled=True)  27.8 us
    pallas_call x1, Pallas kernels, body(): pl.pallas_call(functools.partial(local_kernel, slots, hub_rows), grid=(no...  10.4 us
    all_to_all x2, starting transfers between devices, exchange(): return lax.all_to_all(value, AXES, split_axis=0, concat_axis=0, tiled=True)  9.88 us
    unnamed x32, local copies, waits for them, and re-layouts  9.26 us
    pallas_call x1, Pallas kernels, body(): pl.pallas_call(functools.partial(middle_kernel, fanout, slots), grid=(nod...  9.06 us
    all_to_all x2, waiting for transfers between devices, exchange(): return lax.all_to_all(value, AXES, split_axis=0, concat_axis=0, tiled=True)  5.11 us
    pallas_call x1, Pallas kernels, body(): pl.pallas_call(scatter_kernel, grid=(nodes // block,), in_specs=[full(loc...  4.5 us
    pallas_call x1, Pallas kernels, body(): pl.pallas_call(functools.partial(final_kernel, fanout, slots), grid=(node...  3.64 us
  transfers between devices with their start and end apart: 2, of which 2 were waited for; matrix products, arithmetic and copies ran while one was open for 0% of the time, Pallas kernels for 22%

profile of v1, /device:TPU:0, one launch (start us, length us, event | category | flops | bytes accessed | tf_op | source)
XLA Modules:
  0.0 83.7 jit_solution(769980803171216737)
XLA Ops:
  0.6 0.0 copy-start.4
  0.6 1.2 %copy-done.4 = bf16[2048,256]{1,0:T(8,128)(2,1)S(1)} copy-done((bf16[2048,256]{1,0:T(8,128)(2,1)S(1)}, bf16[2048,256]{1,0:T(8,128)(2,1)}, u32[]{:S(2)}) %copy-start.4) | copy-done | bytes 1048600
  1.9 0.7 copy-done.9
  2.5 0.7 copy-done.15
  3.2 1.5 %pick_rows.1 = bf16[32,32,256]{2,1,0:T(8,128)(2,1)} custom-call(s32[1,512]{1,0:T(1,128)S(1)} %copy-done.9, bf16[2048,256]{1,0:T(8,128)(2,1)S(1)} %copy-done.4, bf16[16,256]{1,0:T(8,128)(2,1)S(1)} %copy-done.15), custom_call_target="tpu_custom_call" | custom-call | flops 536870912 | bytes 1048576 | tf_op jit(solution)/shard_map/pick_rows/pallas_call | solution.py:231
  4.8 7.3 %all-to-all-start = ((bf16[32,32,256]{2,1,0:T(8,128)(2,1)}), bf16[32,32,256]{2,1,0:T(8,128)(2,1)S(1)}, u32[]{:S(2)}, u32[]{:S(2)}) async-start(bf16[32,32,256]{2,1,0:T(8,128)(2,1)} %pick_rows.1), calls=%async_computation | async-start | bytes 1048576 | tf_op jit(solution)/shard_map/all_to_all | solution.py:229
  12.1 0.0 copy-done.12
  12.1 0.0 copy-done.13
  12.1 0.0 copy-done.14
  12.1 0.0 copy-start.5
  12.1 1.2 %copy-done.5 = bf16[2048,256]{1,0:T(8,128)(2,1)S(1)} copy-done((bf16[2048,256]{1,0:T(8,128)(2,1)S(1)}, bf16[2048,256]{1,0:T(8,128)(2,1)}, u32[]{:S(2)}) %copy-start.5) | copy-done | bytes 1048600
  13.4 10.4 %local_gather.1 = (f32[2048,256]{1,0:T(8,128)S(1)}, bf16[2048,1024]{1,0:T(8,128)(2,1)S(1)}, bf16[1024,2048]{1,0:T(8,128)(2,1)}) custom-call(s32[4,2048]{1,0:T(4,128)S(1)} %bitcast.9, s32[2,2048]{1,0:T(2,128)S(1)} %bitcast.11, s32[4,2048]{1,0:T(4,128)S(1)} %bitcast.8, bf16[2048,256]{1,0:T(8,128)(2,1)S(1)} %copy-done.5), custom_call_target="tpu_custom_call" | custom-call | flops 8589934592 | bytes 8388608 | tf_op jit(solution)/shard_map/local_gather/pallas_call | solution.py:241
  23.8 2.0 %copy-done = bf16[2048,1024]{1,0:T(8,128)(2,1)} copy-done((bf16[2048,1024]{1,0:T(8,128)(2,1)}, bf16[2048,1024]{1,0:T(8,128)(2,1)S(1)}, u32[]{:S(2)}) %copy-start) | copy-done | bytes 4194328
  25.8 2.6 %all-to-all-done.table_ref = bf16[32,32,256]{2,1,0:T(8,128)(2,1)S(1)} async-done(((bf16[32,32,256]{2,1,0:T(8,128)(2,1)}), bf16[32,32,256]{2,1,0:T(8,128)(2,1)S(1)}, u32[]{:S(2)}, u32[]{:S(2)}) %all-to-all-start) | async-done | bytes 524320 | tf_op jit(solution)/shard_map/all_to_all | solution.py:229
  28.5 0.0 copy-done.1
  28.5 0.0 copy-done.8
  28.5 0.0 copy-done.11
  28.5 0.0 copy-start.6
  28.5 1.2 %copy-done.6 = bf16[2048,256]{1,0:T(8,128)(2,1)S(1)} copy-done((bf16[2048,256]{1,0:T(8,128)(2,1)S(1)}, bf16[2048,256]{1,0:T(8,128)(2,1)}, u32[]{:S(2)}) %copy-start.6) | copy-done | bytes 1048600
  29.7 1.2 %copy-done.7 = bf16[2048,256]{1,0:T(8,128)(2,1)S(1)} copy-done((bf16[2048,256]{1,0:T(8,128)(2,1)S(1)}, bf16[2048,256]{1,0:T(8,128)(2,1)}, u32[]{:S(2)}) %copy-start.7) | copy-done | bytes 1048600
  30.9 9.1 %activate.1 = (bf16[2048,256]{1,0:T(8,128)(2,1)}, bf16[2048,256]{1,0:T(8,128)(2,1)S(1)}, bf16[32,56,256]{2,1,0:T(8,128)(2,1)S(1)}) custom-call(bf16[2048,256]{1,0:T(8,128)(2,1)S(1)} %copy-done.6, f32[2048,256]{1,0:T(8,128)S(1)} %get-tuple-element.15.sum_ref, bf16[2048,1024]{1,0:T(8,128)(2,1)} %copy-done, bf16[1024,2048]{1,0:T(8,128)(2,1)} %get-tuple-element.17.by_col_ref, ...), custom_call_target="tpu_custom_call" | custom-call | flops 2147483648 | bytes 8388608 | tf_op jit(solution)/shard_map/activate/pallas_call | solution.py:266
  40.0 1.0 %copy-done.2 = bf16[2048,256]{1,0:T(8,128)(2,1)} copy-done((bf16[2048,256]{1,0:T(8,128)(2,1)}, bf16[2048,256]{1,0:T(8,128)(2,1)S(1)}, u32[]{:S(2)}) %copy-start.2) | copy-done | bytes 1048600
  40.9 27.8 %all_to_all.15.back_ref = bf16[32,56,256]{2,1,0:T(8,128)(2,1)S(1)} all-to-all(bf16[32,56,256]{2,1,0:T(8,128)(2,1)S(1)} %get-tuple-element.19), channel_id=1, replica_groups=mesh['row'=4,'col'=8] {'row','col'}, dimensions={0} | all-to-all | bytes 1835008 | tf_op jit(solution)/shard_map/all_to_all | solution.py:229
  68.7 0.8 %sums.1 = (bf16[32,16,256]{2,1,0:T(8,128)(2,1)}, f32[1,256]{1,0:T(1,128)}, f32[16,256]{1,0:T(8,128)}) custom-call(bf16[32,56,256]{2,1,0:T(8,128)(2,1)S(1)} %all_to_all.15.back_ref, bf16[256,256]{1,0:T(8,128)(2,1)S(1)} %copy-done.1), custom_call_target="tpu_custom_call" | custom-call | bytes 1179648 | tf_op jit(solution)/shard_map/sums/pallas_call | solution.py:313
  69.6 2.6 %all-to-all-start.2 = ((bf16[32,16,256]{2,1,0:T(8,128)(2,1)}), bf16[32,16,256]{2,1,0:T(8,128)(2,1)S(1)}, u32[]{:S(2)}, u32[]{:S(2)}) async-start(bf16[32,16,256]{2,1,0:T(8,128)(2,1)} %get-tuple-element.22), calls=%async_computation.2 | async-start | bytes 524288 | tf_op jit(solution)/shard_map/all_to_all | solution.py:229
  72.2 0.0 copy-done.3
  72.2 0.0 copy-start.10
  72.2 4.5 %local_scatter.1.scat_ref = f32[2048,256]{1,0:T(8,128)S(1)} custom-call(s32[4,2048]{1,0:T(4,128)S(1)} %bitcast.10, bf16[2048,256]{1,0:T(8,128)(2,1)S(1)} %copy-done.3), custom_call_target="tpu_custom_call" | custom-call | flops 8589934592 | bytes 3145728 | tf_op jit(solution)/shard_map/local_scatter/pallas_call | solution.py:302
  76.7 0.0 copy-done.10
  76.7 3.6 %return_scatter.1 = f32[2048,256]{1,0:T(8,128)} custom-call(s32[1,512]{1,0:T(1,128)S(1)} %copy-done.10, bf16[32,56,256]{2,1,0:T(8,128)(2,1)S(1)} %all_to_all.15.back_ref, f32[2048,256]{1,0:T(8,128)S(1)} %local_scatter.1.scat_ref, bf16[2048,256]{1,0:T(8,128)(2,1)S(1)} %copy-done.3, bf16[256,256]{1,0:T(8,128)(2,1)S(1)} %copy-done.8, bf16[256,256]{1,0:T(8,128)(2,1)S(1)} %copy-done.1), custom_call_target="tpu_custom_call" | custom-call | flops 536870912 | bytes 5242880 | tf_op jit(solution)/shard_map/return_scatter/pallas_call | solution.py:327
  80.3 2.5 %all-to-all-done.2 = bf16[32,16,256]{2,1,0:T(8,128)(2,1)S(1)} async-done(((bf16[32,16,256]{2,1,0:T(8,128)(2,1)}), bf16[32,16,256]{2,1,0:T(8,128)(2,1)S(1)}, u32[]{:S(2)}, u32[]{:S(2)}) %all-to-all-start.2) | async-done | bytes 262176 | tf_op jit(solution)/shard_map/all_to_all | solution.py:229
  82.8 0.8 %fusion = (f32[16,16,256]{2,1,0:T(8,128)}, f32[16,16,256]{2,1,0:T(8,128)}) fusion(bf16[32,16,256]{2,1,0:T(8,128)(2,1)S(1)} %all-to-all-done.2), kind=kLoop, calls=%fused_computation | loop fusion | bytes 1048576 | tf_op jit(solution)/shard_map/slice | solution.py:346
  (12 shorter events, 0.0 us)
Async XLA Ops:
  0.6 1.2 %copy-start.4 = (bf16[2048,256]{1,0:T(8,128)(2,1)S(1)}, bf16[2048,256]{1,0:T(8,128)(2,1)}, u32[]{:S(2)}) copy-start(bf16[2048,256]{1,0:T(8,128)(2,1)} %feat_ref.5) | copy-start | bytes 3145732
  1.9 0.7 copy-start.9
  2.5 0.7 copy-start.15
  3.2 8.9 %copy-start.12 = (s32[2048,4]{0,1:T(4,128)S(1)}, s32[2048,4]{0,1:T(4,128)}, u32[]{:S(2)}) copy-start(s32[2048,4]{0,1:T(4,128)} %param.17) | copy-start | bytes 98308
  3.2 8.9 %copy-start.13 = (s32[2048,4]{0,1:T(4,128)S(1)}, s32[2048,4]{0,1:T(4,128)}, u32[]{:S(2)}) copy-start(s32[2048,4]{0,1:T(4,128)} %param.15) | copy-start | bytes 98308
  3.2 8.9 %copy-start.14 = (s32[2048,2]{0,1:T(2,128)S(1)}, s32[2048,2]{0,1:T(2,128)}, u32[]{:S(2)}) copy-start(s32[2048,2]{0,1:T(2,128)} %param.16) | copy-start | bytes 49156
  4.8 23.7 %all-to-all-start = ((bf16[32,32,256]{2,1,0:T(8,128)(2,1)}), bf16[32,32,256]{2,1,0:T(8,128)(2,1)S(1)}, u32[]{:S(2)}, u32[]{:S(2)}) async-start(bf16[32,32,256]{2,1,0:T(8,128)(2,1)} %pick_rows.1), calls=%async_computation | async-start | bytes 1048576 | tf_op jit(solution)/shard_map/all_to_all | solution.py:229
  12.1 1.2 %copy-start.5 = (bf16[2048,256]{1,0:T(8,128)(2,1)S(1)}, bf16[2048,256]{1,0:T(8,128)(2,1)}, u32[]{:S(2)}) copy-start(bf16[2048,256]{1,0:T(8,128)(2,1)} %feat_ref.5) | copy-start | bytes 3145732
  13.4 15.1 %copy-start.1 = (bf16[256,256]{1,0:T(8,128)(2,1)S(1)}, bf16[256,256]{1,0:T(8,128)(2,1)}, u32[]{:S(2)}) copy-start(bf16[256,256]{1,0:T(8,128)(2,1)} %wn_ref.5) | copy-start | bytes 393220
  13.4 15.1 %copy-start.8 = (bf16[256,256]{1,0:T(8,128)(2,1)S(1)}, bf16[256,256]{1,0:T(8,128)(2,1)}, u32[]{:S(2)}) copy-start(bf16[256,256]{1,0:T(8,128)(2,1)} %ws_ref.3) | copy-start | bytes 393220
  13.4 15.1 %copy-start.11 = (f32[256]{0:T(256)S(1)}, f32[256]{0:T(256)}, u32[]{:S(2)}) copy-start(f32[256]{0:T(256)} %param.14) | copy-start | bytes 3076
  23.8 2.0 %copy-start = (bf16[2048,1024]{1,0:T(8,128)(2,1)}, bf16[2048,1024]{1,0:T(8,128)(2,1)S(1)}, u32[]{:S(2)}) copy-start(bf16[2048,1024]{1,0:T(8,128)(2,1)S(1)} %get-tuple-element.16.by_row_ref) | copy-start | bytes 12582916
  28.5 1.2 %copy-start.6 = (bf16[2048,256]{1,0:T(8,128)(2,1)S(1)}, bf16[2048,256]{1,0:T(8,128)(2,1)}, u32[]{:S(2)}) copy-start(bf16[2048,256]{1,0:T(8,128)(2,1)} %feat_ref.5) | copy-start | bytes 3145732
  29.7 1.2 %copy-start.7 = (bf16[2048,256]{1,0:T(8,128)(2,1)S(1)}, bf16[2048,256]{1,0:T(8,128)(2,1)}, u32[]{:S(2)}) copy-start(bf16[2048,256]{1,0:T(8,128)(2,1)} %cot_ref.1) | copy-start | bytes 3145732
  40.0 1.0 %copy-start.2 = (bf16[2048,256]{1,0:T(8,128)(2,1)}, bf16[2048,256]{1,0:T(8,128)(2,1)S(1)}, u32[]{:S(2)}) copy-start(bf16[2048,256]{1,0:T(8,128)(2,1)S(1)} %get-tuple-element.20.grad_ref) | copy-start | bytes 3145732
  40.9 31.2 %copy-start.3 = (bf16[2048,256]{1,0:T(8,128)(2,1)S(1)}, bf16[2048,256]{1,0:T(8,128)(2,1)}, u32[]{:S(2)}) copy-start(bf16[2048,256]{1,0:T(8,128)(2,1)} %copy-done.2) | copy-start | bytes 3145732
  69.6 13.2 %all-to-all-start.2 = ((bf16[32,16,256]{2,1,0:T(8,128)(2,1)}), bf16[32,16,256]{2,1,0:T(8,128)(2,1)S(1)}, u32[]{:S(2)}, u32[]{:S(2)}) async-start(bf16[32,16,256]{2,1,0:T(8,128)(2,1)} %get-tuple-element.22), calls=%async_computation.2 | async-start | bytes 524288 | tf_op jit(solution)/shard_map/all_to_all | solution.py:229
  72.2 4.5 %copy-start.10 = (s32[1,512]{1,0:T(1,128)S(1)}, s32[1,512]{1,0:T(1,128)}, u32[]{:S(2)}) copy-start(s32[1,512]{1,0:T(1,128)} %send_ref.3) | copy-start | bytes 6148

commit v2 on v0

v2 whole, which is shorter than its diff:
```python
import functools

import jax
import jax.numpy as jnp
from jax import lax
from jax.experimental import pallas as pl
from jax.experimental.pallas import tpu as pltpu
from jax.sharding import PartitionSpec as P

AXES = ("row", "col")
LANES = 128
TILE = 256
VMEM_LIMIT = 18 * 1024 * 1024
NT = (((1,), (1,)), ((), ()))
TN = (((0,), (0,)), ((), ()))
VMEM = pl.BlockSpec(memory_space=pltpu.VMEM)
SMEM = pl.BlockSpec(memory_space=pltpu.SMEM)
HBM = pl.BlockSpec(memory_space=pltpu.HBM)
bf16, f32 = jnp.bfloat16, jnp.float32


def params():
    return pltpu.CompilerParams(vmem_limit_bytes=VMEM_LIMIT)


def cost(flops, moved):
    return pl.CostEstimate(flops=int(flops), bytes_accessed=int(moved), transcendentals=0)


def along_rows(index_row):
    count = index_row.shape[1]
    return jnp.transpose(jnp.broadcast_to(index_row, (LANES, count))).astype(jnp.int16)


def hits_by_row(columns, first, width):
    rows = columns[0].shape[0]
    lane = lax.broadcasted_iota(jnp.int32, (rows, LANES), 1).astype(jnp.int16)
    one = jnp.ones((rows, LANES), bf16)
    zero = jnp.zeros((rows, LANES), bf16)
    tiles = []
    for start in range(first, first + width, LANES):
        here = lane + jnp.int16(start)
        total = None
        for column in columns:
            hit = jnp.where(column == here, one, zero)
            total = hit if total is None else total + hit
        tiles.append(total)
    return jnp.concatenate(tiles, axis=1) if len(tiles) > 1 else tiles[0]


def hits_by_column(index_rows, first, height):
    count = index_rows[0].shape[1]
    down = lax.broadcasted_iota(jnp.int32, (height, count), 0).astype(jnp.int16)
    one = jnp.ones((height, count), bf16)
    zero = jnp.zeros((height, count), bf16)
    total = None
    for row in index_rows:
        entry = jnp.broadcast_to(row - first, (16, count)).astype(jnp.int16)
        entry = jnp.broadcast_to(entry[None], (height // 16, 16, count)).reshape(height, count)
        hit = jnp.where(entry == down, one, zero)
        total = hit if total is None else total + hit
    return total


def dot(a, b, dims=(((1,), (0,)), ((), ()))):
    return lax.dot_general(a, b, dims, preferred_element_type=f32)


def index_rows(ref, start, count):
    return [ref[j : j + 1, pl.ds(start, count)] for j in range(ref.shape[0])]


def spread_kernel(hub_ref, out_ref):
    out_ref[...] = jnp.broadcast_to(hub_ref[...][None], out_ref.shape)


def pick_kernel(send_ref, feat_hbm, out_ref, feat_ref, sem):
    load = pltpu.make_async_copy(feat_hbm, feat_ref, sem)
    load.start()
    parts, slots, width = out_ref.shape
    total = send_ref.shape[1]
    step = min(512, total)
    load.wait()
    for start in range(0, total, step):
        column = along_rows(send_ref[:, start : start + step])
        picked = dot(hits_by_row([column], 0, feat_ref.shape[0]), feat_ref[...])
        out_ref[start // slots : (start + step) // slots] = picked.astype(bf16).reshape(step // slots, slots, width)


def local_kernel(local_ref, hub_ref, remote_ref, feat_ref, sum_ref, hub_by_row, hub_by_col, rem_by_row, rem_by_col):
    nodes = feat_ref.shape[0]

    @pl.loop(0, nodes // TILE)
    def _(block):
        start = pl.multiple_of(block * TILE, TILE)
        rows = index_rows(local_ref, start, TILE)
        columns = [along_rows(row) for row in rows]
        total = None
        for first in range(0, nodes, TILE):
            part = dot(hits_by_row(columns, first, TILE), feat_ref[first : first + TILE, :])
            total = part if total is None else total + part
        sum_ref[pl.ds(start, TILE), :] = total
        for edge_ref, by_row, by_col in ((remote_ref, rem_by_row, rem_by_col), (hub_ref, hub_by_row, hub_by_col)):
            rows = index_rows(edge_ref, start, TILE)
            columns = [along_rows(row) for row in rows]
            for first in range(0, by_row.shape[1], TILE):
                by_row[pl.ds(start, TILE), first : first + TILE] = hits_by_row(columns, first, TILE)
                by_col[first : first + TILE, pl.ds(start, TILE)] = hits_by_column(rows, first, TILE)


def middle_kernel(
    fanout,
    core_ref,
    feat_ref,
    sum_ref,
    hub_by_row,
    hub_by_col,
    rem_by_row,
    rem_by_col,
    bound_ref,
    hub_ref,
    cot_hbm,
    ws_ref,
    wn_ref,
    bias_ref,
    act_hbm,
    grad_ref,
    bound_out,
    keep_out,
    give_out,
    bias_out,
    cot_ref,
    act_ref,
    mean_ref,
    cot_sem,
    act_sem,
):
    nodes, width = feat_ref.shape
    parts, slots, _ = bound_ref.shape
    hub_rows = hub_ref.shape[1]
    half = hub_rows // 2
    blocks = nodes // TILE
    load = pltpu.make_async_copy(cot_hbm, cot_ref, cot_sem)
    load.start()
    bound = bound_ref[...].reshape(parts * slots, width)
    hubs = hub_ref[...].reshape(parts * hub_rows, width)
    stores = []
    bias_total = jnp.zeros((1, width), f32)
    for block in range(blocks):
        here = slice(block * TILE, (block + 1) * TILE)
        total = sum_ref[here, :] + dot(rem_by_row[here, :], bound) + dot(hub_by_row[here, :], hubs)
        mean = (total / fanout).astype(bf16)
        mean_ref[here, :] = mean
        pre = dot(feat_ref[here, :], ws_ref[...]) + dot(mean, wn_ref[...]) + bias_ref[...]
        sig = jax.nn.sigmoid(pre)
        if block == 0:
            load.wait()
        act_ref[here, :] = (pre * sig).astype(bf16)
        grad = (cot_ref[here, :].astype(f32) * sig * (1.0 + pre * (1.0 - sig))).astype(bf16)
        grad_ref[here, :] = grad
        bias_total = bias_total + jnp.sum(grad.astype(f32), axis=0, keepdims=True)
        store = pltpu.make_async_copy(act_ref.at[here, :], act_hbm.at[here, :], act_sem.at[block])
        store.start()
        stores.append(store)
    grad = grad_ref[...]
    bound_out[...] = dot(rem_by_col[...], grad).astype(bf16).reshape(parts, slots, width)
    hub_terms = dot(hub_by_col[...], grad).reshape(parts, 2, half, width)
    first_core = core_ref[0] == 0
    keep_out[:, :half, :] = jnp.where(first_core, hub_terms[:, 0], hub_terms[:, 1])
    give_out[:, :half, :] = jnp.where(first_core, hub_terms[:, 1], hub_terms[:, 0]).astype(bf16)
    per = width // 16
    for which, source in enumerate((feat_ref, mean_ref)):
        terms = dot(source[...], grad, TN).reshape(per, 2, 8, width)
        held = slice(which * per, (which + 1) * per)
        keep_out[held, half:, :] = jnp.where(first_core, terms[:, 0], terms[:, 1])
        give_out[held, half:, :] = jnp.where(first_core, terms[:, 1], terms[:, 0]).astype(bf16)
    if parts > 2 * per:
        keep_out[2 * per :, half:, :] = jnp.zeros((parts - 2 * per, 8, width), f32)
        give_out[2 * per :, half:, :] = jnp.zeros((parts - 2 * per, 8, width), bf16)
    bias_out[...] = jnp.broadcast_to(bias_total[None], bias_out.shape)
    for store in stores:
        store.wait()


def join_kernel(keep_ref, got_ref, out_ref):
    out_ref[...] = (keep_ref[...] + got_ref[...].astype(f32)).astype(bf16)


def scatter_kernel(local_ref, send_ref, grad_ref, out_ref, hits_ref):
    nodes = out_ref.shape[0]

    @pl.loop(0, nodes // TILE)
    def _(block):
        first = pl.multiple_of(block * TILE, TILE)
        total = None
        for start in range(0, nodes, TILE):
            rows = index_rows(local_ref, start, TILE)
            part = dot(hits_by_column(rows, first, TILE), grad_ref[start : start + TILE, :])
            total = part if total is None else total + part
        out_ref[pl.ds(first, TILE), :] = total
        for start in range(0, send_ref.shape[1], TILE):
            hits_ref[pl.ds(first, TILE), start : start + TILE] = hits_by_column(
                index_rows(send_ref, start, TILE), first, TILE
            )


def sums_kernel(fanout, rows, half, back_ref, wn_ref, weight_ref, hub_ref):
    parts, slab, width = back_ref.shape
    cols = parts // rows
    back = back_ref[...].astype(f32).reshape(rows // 2, 2, cols, slab, width)
    total = jnp.sum(jnp.sum(back, axis=2), axis=0)
    weight = jnp.concatenate([total[0, half:], total[1, half:]], axis=0)
    weight_ref[...] = jnp.broadcast_to(weight.astype(bf16)[None], weight_ref.shape)
    hub = jnp.concatenate([total[0, :half], total[1, :half]], axis=0)
    high = hub.astype(bf16)
    low = (hub - high.astype(f32)).astype(bf16)
    hub_ref[...] = (dot(high, wn_ref[...], NT) + dot(low, wn_ref[...], NT)) / fanout


def final_kernel(fanout, hits_ref, bound_ref, scat_ref, grad_ref, ws_ref, wn_ref, out_hbm, out_ref, sem):
    nodes, width = scat_ref.shape
    returned = bound_ref[...].reshape(hits_ref.shape[1], width)
    stores = []
    for block in range(nodes // TILE):
        here = slice(block * TILE, (block + 1) * TILE)
        total = scat_ref[here, :] + dot(hits_ref[here, :], returned)
        out_ref[here, :] = dot(grad_ref[here, :], ws_ref[...], NT) + dot(
            (total / fanout).astype(bf16), wn_ref[...], NT
        )
        store = pltpu.make_async_copy(out_ref.at[here, :], out_hbm.at[here, :], sem.at[block])
        store.start()
        stores.append(store)
    for store in stores:
        store.wait()


def call(kernel, ins, in_specs, outs, out_specs, scratch, flops, moved, name):
    return pl.pallas_call(
        kernel,
        in_specs=in_specs,
        out_specs=out_specs,
        out_shape=outs,
        scratch_shapes=scratch,
        compiler_params=params(),
        cost_estimate=cost(flops, moved),
        name=name,
    )(*ins)


def body(
    features,
    hub_features,
    w_self,
    w_neigh,
    out_bias,
    local_edges,
    hub_edges,
    remote_edges,
    send_rows,
    cotangent,
):
    nodes, width = features.shape
    hub_rows = hub_features.shape[0]
    half = hub_rows // 2
    rows = lax.axis_size("row")
    parts = lax.axis_size(AXES)
    slots = send_rows.shape[1] // parts
    hubs, bounds = parts * hub_rows, parts * slots
    blocks = nodes // TILE
    fanout = float(local_edges.shape[1] + hub_edges.shape[1] + remote_edges.shape[1])
    local_t, hub_t, remote_t = local_edges.T, hub_edges.T, remote_edges.T
    bias = out_bias.reshape(1, width)
    core = (lax.axis_index("row") % 2).astype(jnp.int32).reshape(1)
    shape = jax.ShapeDtypeStruct

    def exchange(value):
        return lax.all_to_all(value, AXES, split_axis=0, concat_axis=0, tiled=True)

    hub_send = call(
        spread_kernel,
        (hub_features,),
        [VMEM],
        pltpu.HBM((parts, hub_rows, width), bf16),
        pl.BlockSpec((parts, hub_rows, width), lambda: (0, 0, 0)),
        [],
        0,
        hubs * width * 2,
        "spread_hubs",
    )
    hub_all = exchange(hub_send)
    bound_send, feat = call(
        pick_kernel,
        (send_rows, features),
        [VMEM, HBM],
        [pltpu.HBM((parts, slots, width), bf16), pltpu.VMEM((nodes, width), bf16)],
        [pl.BlockSpec((parts, slots, width), lambda: (0, 0, 0)), VMEM],
        [pltpu.SemaphoreType.DMA],
        2 * bounds * nodes * width,
        nodes * width * 2,
        "pick_rows",
    )
    bound_all = exchange(bound_send)

    local_sum, hub_by_row, hub_by_col, rem_by_row, rem_by_col = call(
        local_kernel,
        (local_t, hub_t, remote_t, feat),
        [VMEM] * 4,
        [
            pltpu.VMEM((nodes, width), f32),
            pltpu.VMEM((nodes, hubs), bf16),
            pltpu.VMEM((hubs, nodes), bf16),
            pltpu.VMEM((nodes, bounds), bf16),
            pltpu.VMEM((bounds, nodes), bf16),
        ],
        [VMEM] * 5,
        [],
        8 * nodes * nodes * width,
        nodes * width * 6,
        "local_gather",
    )

    activated, grad_pre, bound_terms, keep, give, bias_rows = call(
        functools.partial(middle_kernel, fanout),
        (
            core,
            feat,
            local_sum,
            hub_by_row,
            hub_by_col,
            rem_by_row,
            rem_by_col,
            bound_all,
            hub_all,
            cotangent,
            w_self,
            w_neigh,
            bias,
        ),
        [SMEM] + [VMEM] * 8 + [HBM] + [VMEM] * 3,
        [
            pltpu.HBM((nodes, width), bf16),
            pltpu.VMEM((nodes, width), bf16),
            pltpu.HBM((parts, slots, width), bf16),
            pltpu.VMEM((parts, half + 8, width), f32),
            pltpu.HBM((parts, half + 8, width), bf16),
            pltpu.HBM((parts, 1, width), f32),
        ],
        [
            HBM,
            VMEM,
            pl.BlockSpec((parts, slots, width), lambda: (0, 0, 0)),
            VMEM,
            pl.BlockSpec((parts, half + 8, width), lambda: (0, 0, 0)),
            pl.BlockSpec((parts, 1, width), lambda: (0, 0, 0)),
        ],
        [
            pltpu.VMEM((nodes, width), bf16),
            pltpu.VMEM((nodes, width), bf16),
            pltpu.VMEM((nodes, width), bf16),
            pltpu.SemaphoreType.DMA,
            pltpu.SemaphoreType.DMA((blocks,)),
        ],
        4 * nodes * (hubs + bounds) * width,
        nodes * width * 8,
        "activate",
    )
    got = lax.ppermute(give, "row", [(r, r ^ 1) for r in range(rows)])
    bound_back = exchange(bound_terms)
    joined = call(
        join_kernel,
        (keep, got),
        [VMEM, VMEM],
        pltpu.HBM((parts, half + 8, width), bf16),
        pl.BlockSpec((parts, half + 8, width), lambda: (0, 0, 0)),
        [],
        0,
        parts * (half + 8) * width * 8,
        "join_siblings",
    )
    sum_back = exchange(joined)
    bias_back = exchange(bias_rows)

    scattered, hits = call(
        scatter_kernel,
        (local_t, send_rows, grad_pre),
        [VMEM] * 3,
        [pltpu.VMEM((nodes, width), f32), pltpu.VMEM((nodes, bounds), bf16)],
        [VMEM] * 2,
        [],
        8 * nodes * nodes * width,
        nodes * width * 6,
        "local_scatter",
    )
    sum_back, scattered = lax.optimization_barrier((sum_back, scattered))

    weight_rows, grad_hubs = call(
        functools.partial(sums_kernel, fanout, rows, half),
        (sum_back, w_neigh),
        [VMEM, VMEM],
        [pltpu.HBM((parts, 16, width), bf16), shape((hub_rows, width), f32)],
        [pl.BlockSpec((parts, 16, width), lambda: (0, 0, 0)), pl.BlockSpec((hub_rows, width), lambda: (0, 0))],
        [],
        0,
        parts * 32 * width * 2,
        "sums",
    )
    weights = exchange(weight_rows)
    grad_bias = jnp.sum(bias_back, axis=(0, 1))

    grad_features = call(
        functools.partial(final_kernel, fanout),
        (hits, bound_back, scattered, grad_pre, w_self, w_neigh),
        [VMEM] * 6,
        pltpu.HBM((nodes, width), f32),
        HBM,
        [pltpu.VMEM((nodes, width), f32), pltpu.SemaphoreType.DMA((blocks,))],
        2 * nodes * bounds * width,
        nodes * width * 10,
        "return_scatter",
    )

    weights = weights[: 2 * width // 16].reshape(2, width, width).astype(f32)
    return (activated, grad_features, grad_hubs, weights[0], weights[1], grad_bias)


def solution(mesh):
    split = P(AXES, None)
    return jax.shard_map(
        body,
        mesh=mesh,
        in_specs=(split, split, P(), P(), P(), split, split, split, split, split),
        out_specs=(split, split, split, P(), P(), P()),
        check_vma=False,
    )
```

time: 355 us -> 112 us (0.32)
  blocking collectives: 116 us -> 13.9 us
  matrix products: 84.6 us -> 0 us
  waiting for transfers between devices: 88.4 us -> 19.4 us
  other arithmetic: 28.7 us -> 1.37 us
  Pallas kernels: 0 us -> 24.1 us
  local copies, waits for them, and re-layouts: 11.3 us -> 29.7 us
  between operations: 14.1 us -> 0.86 us
  starting transfers between devices: 10.1 us -> 21.8 us
    psum x1 -> x0, waiting for transfers between devices: 88.4 us -> none  [body(): hub_summed = lax.psum(hub_terms, ('row', 'col'))]
    dot_general x32 -> x0, matrix products: 84.6 us -> none  [the longest x13 59.4 us: add_transposed(): lax.dot_general(counts, values, (((0,), (0,)), ((), ())), preferred_eleme...]
    all_gather x1 -> x0, blocking collectives: 75 us -> none  [body(): hub_all = lax.all_gather(hub_features, ('row', 'col'), axis=0, tiled=True)]
    psum x1 -> x0, blocking collectives: 40.8 us -> none  [body(): lax.psum((term_self, term_neigh, term_bias), ('row', 'col'))]
    pallas_call x0 -> x8, Pallas kernels: none -> 24.1 us  [call(): pl.pallas_call(kernel, in_specs=in_specs, out_specs=out_specs, out_shape=...]
    unnamed x20 -> x64, local copies, waits for them, and re-layouts: 4 us -> 27.9 us
    reduce_sum x24 -> x1, other arithmetic: 25 us -> 1.37 us  [body(): grad_bias = jnp.sum(bias_back, axis=(0, 1))]
    all_to_all x2 -> x5, waiting for transfers between devices: 0.01 us -> 19.4 us  [exchange(): return lax.all_to_all(value, AXES, split_axis=0, concat_axis=0, tiled=True)]
  transfers between devices with their start and end apart: 3 -> 6, of which waited for: 1 -> 4; matrix products, arithmetic and copies ran while one was open for 3% -> 1% of each run, Pallas kernels for 0% -> 15%
where the time goes in v2:
time: 112 us; the launch traced here: 111 us
  local copies, waits for them, and re-layouts  29.7 us (27%)
  Pallas kernels  24.1 us (22%)
  starting transfers between devices  21.8 us (19%)
  waiting for transfers between devices  19.4 us (17%)
  blocking collectives  13.9 us (12%)
  other arithmetic  1.37 us (1%)
    unnamed x64, local copies, waits for them, and re-layouts  27.9 us
    pallas_call x8, Pallas kernels, call(): pl.pallas_call(kernel, in_specs=in_specs, out_specs=out_specs, out_shape=...  24.1 us
    all_to_all x5, starting transfers between devices, exchange(): return lax.all_to_all(value, AXES, split_axis=0, concat_axis=0, tiled=True)  21.7 us
    all_to_all x5, waiting for transfers between devices, exchange(): return lax.all_to_all(value, AXES, split_axis=0, concat_axis=0, tiled=True)  19.4 us
    all_to_all x1, blocking collectives, exchange(): return lax.all_to_all(value, AXES, split_axis=0, concat_axis=0, tiled=True)  13.9 us
  transfers between devices with their start and end apart: 6, of which 4 were waited for; matrix products, arithmetic and copies ran while one was open for 1% of the time, Pallas kernels for 15%

profile of v2, /device:TPU:0, one launch (start us, length us, event | category | flops | bytes accessed | tf_op | source)
XLA Modules:
  0.0 111.2 jit_solution(12783623353141687131)
XLA Ops:
  2.1 7.3 %all-to-all-start.1 = ((bf16[32,16,256]{2,1,0:T(8,128)(2,1)}), bf16[32,16,256]{2,1,0:T(8,128)(2,1)S(1)}, u32[]{:S(2)}, u32[]{:S(2)}) async-start(bf16[32,16,256]{2,1,0:T(8,128)(2,1)} %spread_hubs.1), calls=%async_computation.1 | async-start | bytes 524288 | tf_op jit(solution)/shard_map/all_to_all | solution.py:277
  9.4 1.2 %copy-done.24 = bf16[2048,256]{1,0:T(8,128)(2,1)S(1)} copy-done((bf16[2048,256]{1,0:T(8,128)(2,1)S(1)}, bf16[2048,256]{1,0:T(8,128)(2,1)}, u32[]{:S(2)}) %copy-start.24) | copy-done | bytes 1048600
  11.3 1.5 %pick_rows.1 = (bf16[32,16,256]{2,1,0:T(8,128)(2,1)}, bf16[2048,256]{1,0:T(8,128)(2,1)S(1)}) custom-call(s32[1,512]{1,0:T(1,128)S(1)} %copy-done.29, bf16[2048,256]{1,0:T(8,128)(2,1)S(1)} %copy-done.24), custom_call_target="tpu_custom_call" | custom-call | flops 536870912 | bytes 1048576 | tf_op jit(solution)/shard_map/pick_rows/pallas_call | solution.py:238
  13.8 6.2 %all-to-all-done.1.hub_ref = bf16[32,16,256]{2,1,0:T(8,128)(2,1)S(1)} async-done(((bf16[32,16,256]{2,1,0:T(8,128)(2,1)}), bf16[32,16,256]{2,1,0:T(8,128)(2,1)S(1)}, u32[]{:S(2)}, u32[]{:S(2)}) %all-to-all-start.1) | async-done | bytes 262176 | tf_op jit(solution)/shard_map/all_to_all | solution.py:277
  20.0 2.6 %all-to-all-start = ((bf16[32,16,256]{2,1,0:T(8,128)(2,1)}), bf16[32,16,256]{2,1,0:T(8,128)(2,1)S(1)}, u32[]{:S(2)}, u32[]{:S(2)}) async-start(bf16[32,16,256]{2,1,0:T(8,128)(2,1)} %get-tuple-element.31), calls=%async_computation | async-start | bytes 524288 | tf_op jit(solution)/shard_map/all_to_all | solution.py:277
  22.6 1.2 %copy-done.16 = bf16[2048,256]{1,0:T(8,128)(2,1)S(1)} copy-done((bf16[2048,256]{1,0:T(8,128)(2,1)S(1)}, bf16[2048,256]{1,0:T(8,128)(2,1)}, u32[]{:S(2)}) %copy-start.16) | copy-done | bytes 1048600
  23.9 7.0 %local_gather.1 = (f32[2048,256]{1,0:T(8,128)S(1)}, bf16[2048,512]{1,0:T(8,128)(2,1)S(1)}, bf16[512,2048]{1,0:T(8,128)(2,1)S(1)}, bf16[2048,512]{1,0:T(8,128)(2,1)S(1)}, bf16[512,2048]{1,0:T(8,128)(2,1)S(1)}) custom-call(s32[4,2048]{1,0:T(4,128)S(1)} %bitcast.9, s32[2,2048]{1,0:T(2,128)S(1)} %bitcast.11, s32[4,2048]{1,0:T(4,128)S(1)} %bitcast.8, ...), custom_call_target="tpu_custom_call" | custom-call | flops 8589934592 | bytes 3145728 | tf_op jit(solution)/shard_map/local_gather/pallas_call | solution.py:238
  30.9 1.3 %copy-done.2 = bf16[2048,512]{1,0:T(8,128)(2,1)} copy-done((bf16[2048,512]{1,0:T(8,128)(2,1)}, bf16[2048,512]{1,0:T(8,128)(2,1)S(1)}, u32[]{:S(2)}) %copy-start.2) | copy-done | bytes 2097176
  32.2 1.3 %copy-done.4 = bf16[512,2048]{1,0:T(8,128)(2,1)} copy-done((bf16[512,2048]{1,0:T(8,128)(2,1)}, bf16[512,2048]{1,0:T(8,128)(2,1)S(1)}, u32[]{:S(2)}) %copy-start.4) | copy-done | bytes 2097176
  33.5 1.3 %copy-done.6 = bf16[2048,512]{1,0:T(8,128)(2,1)} copy-done((bf16[2048,512]{1,0:T(8,128)(2,1)}, bf16[2048,512]{1,0:T(8,128)(2,1)S(1)}, u32[]{:S(2)}) %copy-start.6) | copy-done | bytes 2097176
  34.9 1.4 %copy-done.8 = bf16[512,2048]{1,0:T(8,128)(2,1)} copy-done((bf16[512,2048]{1,0:T(8,128)(2,1)}, bf16[512,2048]{1,0:T(8,128)(2,1)S(1)}, u32[]{:S(2)}) %copy-start.8) | copy-done | bytes 2097176
  36.9 1.6 %copy-done.3 = bf16[2048,512]{1,0:T(8,128)(2,1)S(1)} copy-done((bf16[2048,512]{1,0:T(8,128)(2,1)S(1)}, bf16[2048,512]{1,0:T(8,128)(2,1)}, u32[]{:S(2)}) %copy-start.3) | copy-done | bytes 2097176
  38.5 1.6 %copy-done.5 = bf16[512,2048]{1,0:T(8,128)(2,1)S(1)} copy-done((bf16[512,2048]{1,0:T(8,128)(2,1)S(1)}, bf16[512,2048]{1,0:T(8,128)(2,1)}, u32[]{:S(2)}) %copy-start.5) | copy-done | bytes 2097176
  40.1 1.6 %copy-done.7 = bf16[2048,512]{1,0:T(8,128)(2,1)S(1)} copy-done((bf16[2048,512]{1,0:T(8,128)(2,1)S(1)}, bf16[2048,512]{1,0:T(8,128)(2,1)}, u32[]{:S(2)}) %copy-start.7) | copy-done | bytes 2097176
  41.7 1.6 %copy-done.9 = bf16[512,2048]{1,0:T(8,128)(2,1)S(1)} copy-done((bf16[512,2048]{1,0:T(8,128)(2,1)S(1)}, bf16[512,2048]{1,0:T(8,128)(2,1)}, u32[]{:S(2)}) %copy-start.9) | copy-done | bytes 2097176
  44.3 1.2 %copy-done.14 = bf16[2048,256]{1,0:T(8,128)(2,1)S(1)} copy-done((bf16[2048,256]{1,0:T(8,128)(2,1)S(1)}, bf16[2048,256]{1,0:T(8,128)(2,1)}, u32[]{:S(2)}) %copy-start.14) | copy-done | bytes 1048600
  45.5 1.2 %copy-done.17 = bf16[2048,256]{1,0:T(8,128)(2,1)S(1)} copy-done((bf16[2048,256]{1,0:T(8,128)(2,1)S(1)}, bf16[2048,256]{1,0:T(8,128)(2,1)}, u32[]{:S(2)}) %copy-start.17) | copy-done | bytes 1048600
  47.6 6.7 %activate.1 = (bf16[2048,256]{1,0:T(8,128)(2,1)}, bf16[2048,256]{1,0:T(8,128)(2,1)S(1)}, bf16[32,16,256]{2,1,0:T(8,128)(2,1)}, f32[32,16,256]{2,1,0:T(8,128)S(1)...) custom-call(s32[1]{0:T(128)} %bitcast.core_ref, bf16[2048,256]{1,0:T(8,128)(2,1)S(1)} %copy-done.17, ...), custom_call_target="tpu_custom_call" | custom-call | flops 2147483648 | bytes 4194304 | tf_op jit(solution)/shard_map/activate/pallas_call | solution.py:238
  55.2 5.9 %all-to-all-start.5 = ((f32[32,1,256]{2,1,0:T(1,128)}), f32[32,1,256]{2,1,0:T(1,128)S(1)}, u32[]{:S(2)}, u32[]{:S(2)}) async-start(f32[32,1,256]{2,1,0:T(1,128)} %get-tuple-element.43), calls=%async_computation.5 | async-start | bytes 65536 | tf_op jit(solution)/shard_map/all_to_all | solution.py:277
  61.1 1.0 copy-done.21
  62.9 5.4 %all-to-all-done.5 = f32[32,1,256]{2,1,0:T(1,128)S(1)} async-done(((f32[32,1,256]{2,1,0:T(1,128)}), f32[32,1,256]{2,1,0:T(1,128)S(1)}, u32[]{:S(2)}, u32[]{:S(2)}) %all-to-all-start.5) | async-done | bytes 32800 | tf_op jit(solution)/shard_map/all_to_all | solution.py:277
  68.3 13.9 %all_to_all.30.back_ref = bf16[32,16,256]{2,1,0:T(8,128)(2,1)} all-to-all(bf16[32,16,256]{2,1,0:T(8,128)(2,1)} %join_siblings.1), channel_id=1, replica_groups=mesh['row'=4,'col'=8] {'row','col'}, dimensions={0} | all-to-all | bytes 524288 | tf_op jit(solution)/shard_map/all_to_all | solution.py:277
  82.2 2.6 %all-to-all-start.2 = ((bf16[32,16,256]{2,1,0:T(8,128)(2,1)}), bf16[32,16,256]{2,1,0:T(8,128)(2,1)S(1)}, u32[]{:S(2)}, u32[]{:S(2)}) async-start(bf16[32,16,256]{2,1,0:T(8,128)(2,1)} %get-tuple-element.35), calls=%async_computation.2 | async-start | bytes 524288 | tf_op jit(solution)/shard_map/all_to_all | solution.py:277
  85.6 4.4 %local_scatter.1 = (f32[2048,256]{1,0:T(8,128)S(1)}, bf16[2048,512]{1,0:T(8,128)(2,1)S(1)}) custom-call(s32[4,2048]{1,0:T(4,128)S(1)} %bitcast.10, s32[1,512]{1,0:T(1,128)S(1)} %copy-done.30, bf16[2048,256]{1,0:T(8,128)(2,1)S(1)} %get-tuple-element.33.grad_ref), custom_call_target="tpu_custom_call" | custom-call | flops 8589934592 | bytes 3145728 | tf_op jit(solution)/shard_map/local_scatter/pallas_call | solution.py:238
  90.1 1.3 %copy-done = bf16[2048,512]{1,0:T(8,128)(2,1)} copy-done((bf16[2048,512]{1,0:T(8,128)(2,1)}, bf16[2048,512]{1,0:T(8,128)(2,1)S(1)}, u32[]{:S(2)}) %copy-start) | copy-done | bytes 2097176
  92.2 3.3 %all-to-all-done.2.bound_ref = bf16[32,16,256]{2,1,0:T(8,128)(2,1)S(1)} async-done(((bf16[32,16,256]{2,1,0:T(8,128)(2,1)}), bf16[32,16,256]{2,1,0:T(8,128)(2,1)S(1)}, u32[]{:S(2)}, u32[]{:S(2)}) %all-to-all-start.2) | async-done | bytes 262176 | tf_op jit(solution)/shard_map/all_to_all | solution.py:277
  95.5 3.3 %all-to-all-start.4 = ((bf16[32,16,256]{2,1,0:T(8,128)(2,1)}), bf16[32,16,256]{2,1,0:T(8,128)(2,1)}, u32[]{:S(2)}, u32[]{:S(2)}) async-start(bf16[32,16,256]{2,1,0:T(8,128)(2,1)} %get-tuple-element.42), calls=%async_computation.4 | async-start | bytes 524288 | tf_op jit(solution)/shard_map/all_to_all | solution.py:277
  98.8 1.4 %reduce_sum.9 = f32[256]{0:T(256)} reduce(f32[32,1,256]{2,1,0:T(1,128)} %copy-done.31, f32[]{:T(128)} %constant.19.clone.1), dimensions={0,1}, to_apply=%region_0.1 | reduce | flops 7936 | bytes 33796 | tf_op jit(solution)/shard_map/reduce_sum | solution.py:408
  100.2 1.6 %copy-done.1 = bf16[2048,512]{1,0:T(8,128)(2,1)S(1)} copy-done((bf16[2048,512]{1,0:T(8,128)(2,1)S(1)}, bf16[2048,512]{1,0:T(8,128)(2,1)}, u32[]{:S(2)}) %copy-start.1) | copy-done | bytes 2097176
  102.7 2.2 %return_scatter.1 = f32[2048,256]{1,0:T(8,128)} custom-call(bf16[2048,512]{1,0:T(8,128)(2,1)S(1)} %copy-done.1, bf16[32,16,256]{2,1,0:T(8,128)(2,1)S(1)} %all-to-all-done.2.bound_ref, f32[2048,256]{1,0:T(8,128)S(1)} %get-tuple-element.39.scat_ref, bf16[2048,256]{1,0:T(8,128)(2,1)S(1)} %get-tuple-element.33.grad_ref, bf16[256,256]{1,0:T(8,128)(2,1)S(1)} %copy-done.19, ...), custom_call_target="tpu_custom_call" | custom-call | flops 536870912 | bytes 5242880 | tf_op jit(solution)/shard_map/return_scatter/pallas_call | solution.py:238
  104.9 4.6 %all-to-all-done.4 = bf16[32,16,256]{2,1,0:T(8,128)(2,1)} async-done(((bf16[32,16,256]{2,1,0:T(8,128)(2,1)}), bf16[32,16,256]{2,1,0:T(8,128)(2,1)}, u32[]{:S(2)}, u32[]{:S(2)}) %all-to-all-start.4) | async-done | bytes 262176 | tf_op jit(solution)/shard_map/all_to_all | solution.py:277
  109.4 1.8 %fusion = (f32[16,16,256]{2,1,0:T(8,128)}, f32[16,16,256]{2,1,0:T(8,128)}) fusion(bf16[32,16,256]{2,1,0:T(8,128)(2,1)} %all-to-all-done.4), kind=kLoop, calls=%fused_computation | loop fusion | bytes 1048576 | tf_op jit(solution)/shard_map/slice | solution.py:423
  (55 shorter events, 9.8 us)
Async XLA Ops:
  1.3 21.3 %copy-start.25 = (s32[2048,4]{0,1:T(4,128)S(1)}, s32[2048,4]{0,1:T(4,128)}, u32[]{:S(2)}) copy-start(s32[2048,4]{0,1:T(4,128)} %param.17) | copy-start | bytes 98308
  1.3 21.3 %copy-start.26 = (s32[2048,4]{0,1:T(4,128)S(1)}, s32[2048,4]{0,1:T(4,128)}, u32[]{:S(2)}) copy-start(s32[2048,4]{0,1:T(4,128)} %param.15) | copy-start | bytes 98308
  1.3 21.3 %copy-start.28 = (s32[2048,2]{0,1:T(2,128)S(1)}, s32[2048,2]{0,1:T(2,128)}, u32[]{:S(2)}) copy-start(s32[2048,2]{0,1:T(2,128)} %param.16) | copy-start | bytes 49156
  2.1 18.0 %all-to-all-start.1 = ((bf16[32,16,256]{2,1,0:T(8,128)(2,1)}), bf16[32,16,256]{2,1,0:T(8,128)(2,1)S(1)}, u32[]{:S(2)}, u32[]{:S(2)}) async-start(bf16[32,16,256]{2,1,0:T(8,128)(2,1)} %spread_hubs.1), calls=%async_computation.1 | async-start | bytes 524288 | tf_op jit(solution)/shard_map/all_to_all | solution.py:277
  9.4 1.2 %copy-start.24 = (bf16[2048,256]{1,0:T(8,128)(2,1)S(1)}, bf16[2048,256]{1,0:T(8,128)(2,1)}, u32[]{:S(2)}) copy-start(bf16[2048,256]{1,0:T(8,128)(2,1)} %feat_hbm.1) | copy-start | bytes 3145732
  12.8 1.0 copy-start.15
  20.0 16.2 %all-to-all-start = ((bf16[32,16,256]{2,1,0:T(8,128)(2,1)}), bf16[32,16,256]{2,1,0:T(8,128)(2,1)S(1)}, u32[]{:S(2)}, u32[]{:S(2)}) async-start(bf16[32,16,256]{2,1,0:T(8,128)(2,1)} %get-tuple-element.31), calls=%async_computation | async-start | bytes 524288 | tf_op jit(solution)/shard_map/all_to_all | solution.py:277
  22.6 1.2 %copy-start.16 = (bf16[2048,256]{1,0:T(8,128)(2,1)S(1)}, bf16[2048,256]{1,0:T(8,128)(2,1)}, u32[]{:S(2)}) copy-start(bf16[2048,256]{1,0:T(8,128)(2,1)} %copy-done.15) | copy-start | bytes 3145732
  23.9 13.1 %copy-start.10 = (bf16[256,256]{1,0:T(8,128)(2,1)S(1)}, bf16[256,256]{1,0:T(8,128)(2,1)}, u32[]{:S(2)}) copy-start(bf16[256,256]{1,0:T(8,128)(2,1)} %wn_ref.5) | copy-start | bytes 393220
  23.9 13.1 %copy-start.23 = (f32[256]{0:T(256)S(1)}, f32[256]{0:T(256)}, u32[]{:S(2)}) copy-start(f32[256]{0:T(256)} %param.14) | copy-start | bytes 3076
  30.9 1.3 %copy-start.2 = (bf16[2048,512]{1,0:T(8,128)(2,1)}, bf16[2048,512]{1,0:T(8,128)(2,1)S(1)}, u32[]{:S(2)}) copy-start(bf16[2048,512]{1,0:T(8,128)(2,1)S(1)} %get-tuple-element.27.hub_by_row) | copy-start | bytes 6291460
  32.2 1.3 %copy-start.4 = (bf16[512,2048]{1,0:T(8,128)(2,1)}, bf16[512,2048]{1,0:T(8,128)(2,1)S(1)}, u32[]{:S(2)}) copy-start(bf16[512,2048]{1,0:T(8,128)(2,1)S(1)} %get-tuple-element.28.hub_by_col) | copy-start | bytes 6291460
  33.5 1.3 %copy-start.6 = (bf16[2048,512]{1,0:T(8,128)(2,1)}, bf16[2048,512]{1,0:T(8,128)(2,1)S(1)}, u32[]{:S(2)}) copy-start(bf16[2048,512]{1,0:T(8,128)(2,1)S(1)} %get-tuple-element.29.rem_by_row) | copy-start | bytes 6291460
  34.9 1.4 %copy-start.8 = (bf16[512,2048]{1,0:T(8,128)(2,1)}, bf16[512,2048]{1,0:T(8,128)(2,1)S(1)}, u32[]{:S(2)}) copy-start(bf16[512,2048]{1,0:T(8,128)(2,1)S(1)} %get-tuple-element.30.rem_by_col) | copy-start | bytes 6291460
  36.9 1.6 %copy-start.3 = (bf16[2048,512]{1,0:T(8,128)(2,1)S(1)}, bf16[2048,512]{1,0:T(8,128)(2,1)}, u32[]{:S(2)}) copy-start(bf16[2048,512]{1,0:T(8,128)(2,1)} %copy-done.2) | copy-start | bytes 6291460
  38.5 1.6 %copy-start.5 = (bf16[512,2048]{1,0:T(8,128)(2,1)S(1)}, bf16[512,2048]{1,0:T(8,128)(2,1)}, u32[]{:S(2)}) copy-start(bf16[512,2048]{1,0:T(8,128)(2,1)} %copy-done.4) | copy-start | bytes 6291460
  40.1 1.6 %copy-start.7 = (bf16[2048,512]{1,0:T(8,128)(2,1)S(1)}, bf16[2048,512]{1,0:T(8,128)(2,1)}, u32[]{:S(2)}) copy-start(bf16[2048,512]{1,0:T(8,128)(2,1)} %copy-done.6) | copy-start | bytes 6291460
  41.7 1.6 %copy-start.9 = (bf16[512,2048]{1,0:T(8,128)(2,1)S(1)}, bf16[512,2048]{1,0:T(8,128)(2,1)}, u32[]{:S(2)}) copy-start(bf16[512,2048]{1,0:T(8,128)(2,1)} %copy-done.8) | copy-start | bytes 6291460
  43.3 0.9 copy-start.12
  44.3 1.2 %copy-start.14 = (bf16[2048,256]{1,0:T(8,128)(2,1)S(1)}, bf16[2048,256]{1,0:T(8,128)(2,1)}, u32[]{:S(2)}) copy-start(bf16[2048,256]{1,0:T(8,128)(2,1)} %cot_hbm.1) | copy-start | bytes 3145732
  45.5 1.2 %copy-start.17 = (bf16[2048,256]{1,0:T(8,128)(2,1)S(1)}, bf16[2048,256]{1,0:T(8,128)(2,1)}, u32[]{:S(2)}) copy-start(bf16[2048,256]{1,0:T(8,128)(2,1)} %copy-done.15) | copy-start | bytes 3145732
  55.1 29.7 %copy-start.30 = (s32[1,512]{1,0:T(1,128)S(1)}, s32[1,512]{1,0:T(1,128)}, u32[]{:S(2)}) copy-start(s32[1,512]{1,0:T(1,128)} %send_ref.3) | copy-start | bytes 6148
  55.1 6.0 %collective-permute-start = (bf16[32,16,256]{2,1,0:T(8,128)(2,1)}, bf16[32,16,256]{2,1,0:T(8,128)(2,1)S(1)}, u32[]{:S(2)}, u32[]{:S(2)}) collective-permute-start(bf16[32,16,256]{2,1,0:T(8,128)(2,1)} %get-tuple-element.37), channel_id=1, source_target_pairs={{0,8},{8,0},{16,24},{24,16},{1,9},{9,1},{17,25},{25,17},{2,10},{10... | collective-permute-start | bytes 786440 | tf_op jit(solution)/shard_map/ppermute | solution.py:367
  55.2 13.1 %all-to-all-start.5 = ((f32[32,1,256]{2,1,0:T(1,128)}), f32[32,1,256]{2,1,0:T(1,128)S(1)}, u32[]{:S(2)}, u32[]{:S(2)}) async-start(f32[32,1,256]{2,1,0:T(1,128)} %get-tuple-element.43), calls=%async_computation.5 | async-start | bytes 65536 | tf_op jit(solution)/shard_map/all_to_all | solution.py:277
  61.1 1.0 copy-start.21
  68.3 13.9 %copy-start.31 = (f32[32,1,256]{2,1,0:T(1,128)}, f32[32,1,256]{2,1,0:T(1,128)S(1)}, u32[]{:S(2)}) copy-start(f32[32,1,256]{2,1,0:T(1,128)S(1)} %all-to-all-done.5) | copy-start | bytes 98308
  82.2 13.2 %all-to-all-start.2 = ((bf16[32,16,256]{2,1,0:T(8,128)(2,1)}), bf16[32,16,256]{2,1,0:T(8,128)(2,1)S(1)}, u32[]{:S(2)}, u32[]{:S(2)}) async-start(bf16[32,16,256]{2,1,0:T(8,128)(2,1)} %get-tuple-element.35), calls=%async_computation.2 | async-start | bytes 524288 | tf_op jit(solution)/shard_map/all_to_all | solution.py:277
  85.6 5.8 %copy-start.13 = (bf16[32,16,256]{2,1,0:T(8,128)(2,1)S(1)}, bf16[32,16,256]{2,1,0:T(8,128)(2,1)}, u32[]{:S(2)}) copy-start(bf16[32,16,256]{2,1,0:T(8,128)(2,1)} %all_to_all.30.back_ref) | copy-start | bytes 786436
  90.1 1.3 %copy-start = (bf16[2048,512]{1,0:T(8,128)(2,1)}, bf16[2048,512]{1,0:T(8,128)(2,1)S(1)}, u32[]{:S(2)}) copy-start(bf16[2048,512]{1,0:T(8,128)(2,1)S(1)} %get-tuple-element.34.hits_ref) | copy-start | bytes 6291460
  95.5 13.9 %all-to-all-start.4 = ((bf16[32,16,256]{2,1,0:T(8,128)(2,1)}), bf16[32,16,256]{2,1,0:T(8,128)(2,1)}, u32[]{:S(2)}, u32[]{:S(2)}) async-start(bf16[32,16,256]{2,1,0:T(8,128)(2,1)} %get-tuple-element.42), calls=%async_computation.4 | async-start | bytes 524288 | tf_op jit(solution)/shard_map/all_to_all | solution.py:277
  100.2 1.6 %copy-start.1 = (bf16[2048,512]{1,0:T(8,128)(2,1)S(1)}, bf16[2048,512]{1,0:T(8,128)(2,1)}, u32[]{:S(2)}) copy-start(bf16[2048,512]{1,0:T(8,128)(2,1)} %copy-done) | copy-start | bytes 6291460
  101.8 0.9 copy-start.19
  (6 other events, 4.5 us)
